TPU v7x, 256 devices: a whole 4x4x8 slice. The times are simulated.
256 devices in a mesh: band: 64 (over x, z, core), grp: 4 (over y).
Axes of the slice: x: 4, y: 4, z: 8, core: 2. Of those that a mesh axis runs over, the one named last changes fastest.
Arguments:
- stick_data: bfloat16 [192, 64, 6400], P('band'), may hold values from -6 to 6
- row_lengths: int32 [64], replicated, may hold values from 1 to 3, 80 in all
- row_order: int32 [80], replicated, may hold values from 0 to 79, each once
- source_order: int32 [64], replicated, may hold values from 0 to 63, each once
Outputs:
- exchange_sticks: bfloat16 [192, 64, 6400], P('band')
Inputs may be any that keep to these rules, and one draw needn't show every extreme that they name: `row_lengths`: counts of G-stick rows per device sum to 80; the busiest device holds exactly 3. `row_order`: each G-stick row appears once. `source_order`: each orbital appears once; group g takes the entries g * 4 to g * 4 + 3.
All inputs are finite; a program needn't handle non-finite values.
Results may differ from a plain program's by a relative error of at most 0.019.
Values may be sent and summed in bfloat16 or wider, within the bound.
No kernel may reach another device: no remote copies, remote signals or barrier semaphores. Data moves between devices by JAX's collectives and lax.ppermute only.
A program may use at most 64 MiB of HBM per device.

v0:
```python
import math

import jax
import jax.numpy as jnp
from jax import lax
from jax.sharding import PartitionSpec as P

NGX = 80
NGY = 80
NGZ = 80
SRC = 4


coulomb_peak = 4.0
screen_square = 64.0


def broadcast(block, axis, source):
    block = jnp.where(lax.axis_index(axis) == source, block, jnp.zeros_like(block))
    return lax.psum(block, axis)


def hartley(length):
    indices = jnp.arange(length, dtype=jnp.int32)
    product = indices[:, None] * indices[None, :] % length
    angles = product.astype(jnp.float32) * (2.0 * math.pi / length)
    return ((jnp.cos(angles) + jnp.sin(angles)) / math.sqrt(length)).astype(jnp.bfloat16)


def folded(length):
    indices = jnp.arange(length, dtype=jnp.int32)
    return jnp.minimum(indices, length - indices).astype(jnp.float32)


def screen_kernel():
    freq_x = folded(NGX)
    freq_y = folded(NGY)
    freq_z = folded(NGZ)
    square = (
        (freq_x * freq_x)[:, None, None]
        + (freq_y * freq_y)[None, :, None]
        + (freq_z * freq_z)[None, None, :]
    )
    return coulomb_peak / (1.0 + square / screen_square)


def transform(values, tables, keep_float):
    table_x, table_y, table_z = tables
    values = jnp.einsum(
        "kx,bxyz->bkyz", table_x, values, preferred_element_type=jnp.float32
    ).astype(jnp.bfloat16)
    values = jnp.einsum(
        "ky,bxyz->bxkz", table_y, values, preferred_element_type=jnp.float32
    ).astype(jnp.bfloat16)
    values = jnp.einsum("kz,bxyz->bxyk", table_z, values, preferred_element_type=jnp.float32)
    if keep_float:
        return values
    return values.astype(jnp.bfloat16)


def shards(stick_data, row_lengths, row_order, source_order):
    capacity = stick_data.shape[0]
    orbit_count = stick_data.shape[1]
    plane_size = stick_data.shape[2]
    band_count = lax.axis_size("band")
    per_device = orbit_count // band_count
    slot_count = band_count * capacity
    slot_index = jnp.arange(slot_count, dtype=jnp.int32)
    owner_band = slot_index // capacity
    within = slot_index % capacity
    starts = jnp.cumsum(row_lengths) - row_lengths
    is_live = within < row_lengths[owner_band]
    position = jnp.clip(starts[owner_band] + within, 0, NGX - 1)
    row_of_slot = row_order[position]
    grid_rows = jnp.arange(NGX, dtype=jnp.int32)
    selector = ((row_of_slot[None, :] == grid_rows[:, None]) & is_live[None, :]).astype(
        jnp.bfloat16
    )
    group_index = lax.axis_index("grp")
    received = lax.all_to_all(stick_data, "band", split_axis=1, concat_axis=0, tiled=True)
    coeffs = jnp.einsum(
        "rs,stp->trp", selector, received, preferred_element_type=jnp.float32
    ).astype(jnp.bfloat16)
    tables = (hartley(NGX), hartley(NGY), hartley(NGZ))
    kernel = screen_kernel()
    orbitals = transform(coeffs.reshape(per_device, NGX, NGY, NGZ), tables, False)
    chosen = lax.dynamic_slice_in_dim(source_order, group_index * SRC, SRC, 0)
    partial_value = jnp.zeros((per_device, NGX, NGY, NGZ), jnp.float32)
    for source_slot in range(SRC):
        source_band = chosen[source_slot]
        own_orbital = lax.dynamic_index_in_dim(
            orbitals, source_band % per_device, 0, keepdims=False
        )
        source = broadcast(own_orbital, "band", source_band // per_device)
        density = (orbitals.astype(jnp.float32) * source.astype(jnp.float32)[None]).astype(
            jnp.bfloat16
        )
        spectrum = transform(density, tables, False)
        filtered = (kernel[None] * spectrum.astype(jnp.float32)).astype(jnp.bfloat16)
        potential = transform(filtered, tables, False)
        partial_value = partial_value + source.astype(jnp.float32)[None] * potential.astype(
            jnp.float32
        )
    spectrum_part = transform(partial_value.astype(jnp.bfloat16), tables, True).reshape(
        per_device, NGX, plane_size
    )
    summed = lax.psum(spectrum_part.astype(jnp.bfloat16), "grp")
    outgoing = jnp.einsum(
        "rs,trp->stp", selector, summed, preferred_element_type=jnp.float32
    ).astype(jnp.bfloat16)
    return lax.all_to_all(outgoing, "band", split_axis=0, concat_axis=1, tiled=True)


def solution(mesh):
    return jax.shard_map(
        shards,
        mesh=mesh,
        in_specs=(P("band", None, None), P(), P(), P()),
        out_specs=P("band", None, None),
        check_vma=False,
    )
```

profile of v0, /device:TPU:1, one launch (start us, length us, event | category | flops | bytes accessed | tf_op | source)
XLA Modules:
  0.0 614.5 jit_solution(5159050470298943902)
XLA Ops:
  6.5 5.5 copy.47
  12.0 13.1 %all-to-all-start = ((bf16[3,64,6400]{2,0,1:T(4,128)(2,1)}), bf16[3,64,6400]{2,0,1:T(4,128)(2,1)S(1)}, u32[]{:S(2)}, u32[]{:S(2)}) async-start(bf16[3,64,6400]{2,0,1:T(4,128)(2,1)} %copy.47), calls=%async_computation | async-start | bytes 6553600 | tf_op jit(solution)/shard_map/all_to_all | solution.py:80
  33.5 68.0 %all-to-all-done = bf16[3,64,6400]{2,0,1:T(4,128)(2,1)S(1)} async-done(((bf16[3,64,6400]{2,0,1:T(4,128)(2,1)}), bf16[3,64,6400]{2,0,1:T(4,128)(2,1)S(1)}, u32[]{:S(2)}, u32[]{:S(2)}) %all-to-all-start) | async-done | bytes 2457632 | tf_op jit(solution)/shard_map/all_to_all | solution.py:80
  101.5 4.2 reshape.377
  109.5 4.3 copy.49
  113.9 4.4 broadcast_select_fusion
  118.4 196.9 %all-reduce.6.cloned.1.call-done = (bf16[80,80,80]{2,1,0:T(8,128)(2,1)}, bf16[80,80,80]{2,1,0:T(8,128)(2,1)}, bf16[80,80,80]{2,1,0:T(8,128)(2,1)}, bf16[80,80,80]{2,1,0:T(8,128)(2,1)}) async-done(((bf16[80,80,80]{2,1,0:T(8,128)(2,1)}, bf16[80,80,80]{2,1,0:T(8,128)(2,1)}, bf16[80,80,80]{2,1,0:T(8,128)(2,1)}, bf16[80,80,80]{2,1,0:T(8,128)(2,1)}), (bf16[80,80,80]{2,1,0:T(8,128)(2,1)}, ...) | async-done | bytes 4096016 | tf_op jit(solution)/shard_map/psum | solution.py:20
  315.3 5.9 fusion.6
  323.3 6.0 copy.64
  332.8 4.8 copy.65
  337.6 4.9 fusion.43
  342.4 5.9 copy.67
  348.3 3.9 convolution_convert_fusion.11
  352.3 3.5 fusion.26
  355.8 5.8 copy.58
  365.1 4.9 copy.59
  370.0 4.9 fusion.42
  374.9 5.8 copy.61
  380.7 4.1 convolution_convert_fusion.17
  386.7 5.4 copy.70
  394.0 4.0 copy.71
  401.4 5.8 copy.73
  410.5 4.3 copy.52
  422.5 6.0 copy.55
  428.6 7.4 %fusion.5 = bf16[80,80,80]{2,1,0:T(8,128)(2,1)} fusion(bf16[80,80,80]{2,1,0:T(8,128)(2,1)S(1)} %copy-done.3, bf16[80,80,80]{2,1,0:T(8,128)(2,1)S(1)} %copy-done.4, bf16[80,80,80]{2,1,0:T(8,128)(2,1)} %get-tuple-element.7, bf16[80,80,80]{2,1,0:T(8,128)(2,1)} %get-tuple-element.8, bf16[80,80,80]{2,1,0:T(8,128)(2,1)} %convolution_convert_fusion.5, ...), kind=kOutput, calls=%fused_computation.18 | convolution fusion | flops 173209600 | bytes 9216000 | tf_op jit(solution)/shard_map/kz,bxyz->bxyk/dot_general | solution.py:55
  438.2 4.5 copy.76
  446.6 49.8 %all-reduce.4.cloned.1.call-done = bf16[80,6400]{1,0:T(8,128)(2,1)} async-done(((bf16[80,6400]{1,0:T(8,128)(2,1)}), bf16[80,6400]{1,0:T(8,128)(2,1)}) %all-reduce.4.cloned.1.call-update) | async-done | bytes 1024016 | tf_op jit(solution)/shard_map/psum | solution.py:107
  502.3 4.6 reshape.428
  506.9 71.3 %all_to_all.33 = bf16[64,2,9600]{2,1,0:T(2,128)(2,1)S(1)} all-to-all(bf16[64,2,9600]{2,1,0:T(2,128)(2,1)} %reshape.428), channel_id=1, replica_groups=mesh['band'=64,'grp'=4] {'band'}, dimensions={0} | all-to-all | bytes 4915200 | tf_op jit(solution)/shard_map/all_to_all | solution.py:111
  578.2 6.8 %reshape.429 = bf16[192,1,6400]{2,1,0:T(2,128)(2,1)} reshape(bf16[64,2,9600]{2,1,0:T(2,128)(2,1)S(1)} %all_to_all.33) | data formatting | bytes 4915200
  585.0 16.1 %reduce.1 = bf16[192,6400]{1,0:T(8,128)(2,1)} reduce(bf16[192,1,6400]{2,1,0:T(2,128)(2,1)} %reshape.429, bf16[]{:T(256)} %constant.137), dimensions={1}, to_apply=%all_to_all.27.reduce_sub_computation | reduce | bytes 4915202 | tf_op jit(solution)/shard_map/all_to_all | solution.py:111
  601.1 4.7 all_to_all.28
  (53 shorter events, 50.6 us)
Async XLA Ops:
  6.5 25.4 %copy-start = (s32[80]{0:T(128)S(1)}, s32[80]{0:T(128)}, u32[]{:S(2)}) copy-start(s32[80]{0:T(128)} %param.6) | copy-start | bytes 964
  12.0 13.2 %copy-start.5 = (s32[64]{0:T(128)S(1)}, s32[64]{0:T(128)}, u32[]{:S(2)}) copy-start(s32[64]{0:T(128)} %param.7) | copy-start | bytes 772
  12.0 16.4 %copy-start.2 = (s32[64]{0:T(128)S(1)}, s32[64]{0:T(128)}, u32[]{:S(2)}) copy-start(s32[64]{0:T(128)} %param.5) | copy-start | bytes 772
  12.0 89.4 %all-to-all-start = ((bf16[3,64,6400]{2,0,1:T(4,128)(2,1)}), bf16[3,64,6400]{2,0,1:T(4,128)(2,1)S(1)}, u32[]{:S(2)}, u32[]{:S(2)}) async-start(bf16[3,64,6400]{2,0,1:T(4,128)(2,1)} %copy.47), calls=%async_computation | async-start | bytes 6553600 | tf_op jit(solution)/shard_map/all_to_all | solution.py:80
  25.2 290.2 %all-reduce.6.cloned.1.call-start = ((), (), s32[]{:S(2)}) async-start(), calls=%async_computation.3 | async-start | bytes 13107200 | tf_op jit(solution)/shard_map/psum | solution.py:20
  118.3 378.2 %all-reduce.4.cloned.1.call-start = ((), (), s32[]{:S(2)}) async-start(), calls=%async_computation.2 | async-start | bytes 2048000 | tf_op jit(solution)/shard_map/psum | solution.py:107
  422.5 6.0 copy-start.3
  422.5 6.0 copy-start.4
  605.8 1.7 copy-start.1
Sparse Core Ops, SparseCore 0:
  118.4 196.8 all-reduce.5
  446.8 49.6 all-reduce.3
where the time goes:
time: 623 us; the launch traced here: 615 us
  waiting for transfers between devices  315 us (51%)
  local copies, waits for them, and re-layouts  108 us (17%)
  blocking collectives  71.3 us (11%)
  matrix products  65.3 us (10%)
  other arithmetic  25.6 us (4%)
  between operations  16.3 us (3%)
  starting transfers between devices  13.2 us (2%)
    psum x1, waiting for transfers between devices, broadcast(): return lax.psum(block, axis)  197 us
    another operation x18, local copies, waits for them, and re-layouts  78.9 us
    all_to_all x1, blocking collectives, shards(): lax.all_to_all(outgoing, 'band', split_axis=0, concat_axis=1, tiled=True)  71.3 us
    all_to_all x1, waiting for transfers between devices, shards(): lax.all_to_all(stick_data, 'band', split_axis=1, concat_axis=0, tiled=True)  68 us
    psum x1, waiting for transfers between devices, shards(): summed = lax.psum(spectrum_part.astype(jnp.bfloat16), 'grp')  49.8 us
    dot_general x10, matrix products, transform(): jnp.einsum('kx,bxyz->bkyz', table_x, values, preferred_element_type=jnp.f...  27.9 us
    dot_general x6, matrix products, transform(): jnp.einsum('kz,bxyz->bxyk', table_z, values, preferred_element_type=jnp.f...  23.6 us
    unnamed x15, local copies, waits for them, and re-layouts  16.9 us
  transfers between devices with their start and end apart: 3, of which 3 were waited for; matrix products, arithmetic and copies ran while one was open for 1% of the time, Pallas kernels for 0%

commit v1 on v0

v1 whole, which is shorter than its diff:
```python
import math

import jax
import jax.numpy as jnp
import numpy as np
from jax import lax
from jax.experimental import pallas as pl
from jax.experimental.pallas import tpu as pltpu
from jax.sharding import PartitionSpec as P

N = 80
LANES = 128
TILES = 50
QUART = 13
SRC = 4
SLOTS = 3
BANDS = 64
GROUPS = 4
ROWS_T = 40
ROWS_S = 16
PITCH = 80
BF = jnp.bfloat16
F32 = jnp.float32

coulomb_peak = 4.0
screen_square = 64.0


def hartley_table():
    index = np.arange(N)
    angles = (index[:, None] * index[None, :] % N).astype(np.float32) * np.float32(2.0 * math.pi / N)
    return ((np.cos(angles) + np.sin(angles)) / np.float32(math.sqrt(N))).astype(BF)


def expand_tables(table):
    out = np.zeros((4, 256, 256), BF)
    for p in range(4):
        off = 160 * p % LANES
        out[p, off : off + N, :N] = table
        out[p, off + N : off + 2 * N, LANES : LANES + N] = table
    return out


def pair_table(table):
    out = np.zeros((256, 256), BF)
    out[:N, :N] = table
    out[LANES : LANES + N, LANES : LANES + N] = table
    return out


def compress_tables(table):
    whole = np.zeros((1024, 640), BF)
    for y in range(8):
        whole[y * LANES : y * LANES + N, y * N : (y + 1) * N] = table
    return whole[:512, :256].copy(), whole[384:896, 256:512].copy(), whole[768:, 512:].copy()


def screen_table():
    freq = np.minimum(np.arange(N), N - np.arange(N)).astype(np.float32)
    sq = freq * freq
    total = sq[:41, None, None] + sq[None, :, None] + sq[None, None, :]
    out = np.zeros((41, N, LANES), np.float32)
    out[:, :, :N] = np.float32(coulomb_peak) / (np.float32(1.0) + total / np.float32(screen_square))
    return out


def dot(a, b):
    return jnp.dot(a, b, preferred_element_type=F32)


def dot_tn(a, b):
    return lax.dot_general(a, b, (((0,), (0,)), ((), ())), preferred_element_type=F32)


def pack_kernel(order_s, stick, lengths, order_v, table, msg_t, msg_s, sel, sel_t, scr, scr_s):
    g = lax.axis_index("grp")
    lens = lengths[...]
    d0 = lax.broadcasted_iota(jnp.int32, (BANDS, BANDS), 0)
    d1 = lax.broadcasted_iota(jnp.int32, (BANDS, BANDS), 1)
    before = jnp.where(d0 < d1, 1.0, 0.0).astype(BF)
    lens8 = jnp.broadcast_to(lens, (8, BANDS)).astype(F32)
    starts = dot(lens8.astype(BF), before)[:1]
    q0 = lax.broadcasted_iota(jnp.int32, (N, N), 0)
    perm = jnp.where(jnp.broadcast_to(order_v[...], (N, N)) == q0, 1.0, 0.0).astype(BF)
    permuted = dot(table[...], perm).astype(BF)
    place = lax.broadcasted_iota(jnp.int32, (N, BANDS), 0).astype(F32)
    for c in range(SLOTS):
        hit = (place == jnp.broadcast_to(starts + c, (N, BANDS))) & (
            jnp.broadcast_to(lens8[:1], (N, BANDS)) > c
        )
        one = jnp.where(hit, 1.0, 0.0).astype(BF)
        sel[c] = dot(permuted, one).astype(BF)
        sel_t[c] = lax.dot_general(
            one, permuted, (((0,), (1,)), ((), ())), preferred_element_type=F32
        ).astype(BF)
    first = QUART * g
    for c in range(SLOTS):

        def body(t, _):
            lane = pl.multiple_of(jnp.minimum(first + t, TILES - 1) * LANES, LANES)
            row = pl.multiple_of((c * QUART + t) * BANDS, BANDS)
            scr[pl.ds(row, BANDS), :] = stick[c, :, pl.ds(lane, LANES)].astype(F32)
            return 0

        lax.fori_loop(0, QUART, body, 0, unroll=True)

    def out_body(b, _):
        msg_t[b] = scr[pl.ds(b, ROWS_T, stride=BANDS), :].astype(BF)
        return 0

    lax.fori_loop(0, BANDS, out_body, 0, unroll=8)
    b1 = lax.broadcasted_iota(jnp.int32, (16, BANDS), 1)
    r1 = lax.broadcasted_iota(jnp.int32, (16, BANDS), 0)
    pick = jnp.zeros((16, BANDS), F32)
    for k in range(SRC):
        pick = jnp.where((r1 == k) & (b1 == order_s[g * SRC + k]), 1.0, pick)
    pick = pick.astype(BF)
    for c in range(SLOTS):
        for u in range(TILES // 2):
            got = dot(pick, stick[c, :, u * 256 : u * 256 + 256])
            for h in range(2):
                row = (2 * u + h) * ROWS_S + c * SRC
                scr_s[row : row + SRC, :] = got[:SRC, h * LANES : (h + 1) * LANES]
    for t in range(TILES):
        msg_s[t] = scr_s[t * ROWS_S : (t + 1) * ROWS_S, :].astype(BF)


def rows_kernel(got_t, got_s, sel, quarter, piece, scr, scr_s):
    def load(d, _):
        scr[pl.ds(pl.multiple_of(d * ROWS_T, 8), ROWS_T), :] = got_t[d].astype(F32)
        scr_s[pl.ds(pl.multiple_of(d * ROWS_S, 8), ROWS_S), :] = got_s[d].astype(F32)
        return 0

    lax.fori_loop(0, BANDS, load, 0, unroll=8)
    tables = [sel[c] for c in range(SLOTS)]
    for t in range(QUART):
        total = jnp.zeros((N, LANES), F32)
        for c in range(SLOTS):
            rows = scr[pl.ds(c * QUART + t, BANDS, stride=ROWS_T), :].astype(BF)
            total = total + dot(tables[c], rows)
        quarter[t] = total.astype(BF)
    for k in range(SRC):
        total = jnp.zeros((N, LANES), F32)
        for c in range(SLOTS):
            rows = scr_s[pl.ds(c * SRC + k, BANDS, stride=ROWS_S), :].astype(BF)
            total = total + dot(tables[c], rows)
        piece[k] = total.astype(BF)


def turned(scr, index):
    return jnp.concatenate(
        [
            scr[pl.ds(index, N, stride=PITCH), :].astype(BF),
            scr[pl.ds(index + 1, N, stride=PITCH), :].astype(BF),
        ],
        axis=1,
    )


def put(scr, index, values):
    scr[pl.ds(pl.multiple_of(index * PITCH, 8), N), :] = values[:, :LANES]
    scr[pl.ds(pl.multiple_of(index * PITCH + PITCH, 8), N), :] = values[:, LANES:]


def to_real(tile, out, table, expand, scr):
    def z_body(i, _):
        for p in range(4):
            a = i * 5 + (160 * p) // LANES
            both = jnp.concatenate([tile(a), tile(a + 1)], axis=1)
            put(scr, i * 8 + 2 * p, dot(both, expand[p]))
        return 0

    lax.fori_loop(0, 10, z_body, 0)
    h = table[...]

    def y_body(i, _):
        for p in range(4):
            x = i * 8 + 2 * p
            res = dot(h, turned(scr, x)).astype(BF)
            out[x] = res[:, :LANES]
            out[x + 1] = res[:, LANES:]
        return 0

    lax.fori_loop(0, 10, y_body, 0)


def pairs_kernel(
    quarters, same_core, other_core, table, expand, twin, c0, c1, c2, screen,
    out0, out1, out2, out3,
    target, source, partial, scr_a, scr_b, final, pieces,
):
    g = lax.axis_index("grp")
    band = lax.axis_index("band")
    core, z_at, x_at = band & 1, (band >> 1) & 7, band >> 4
    for kx in range(4):
        for kz in range(8):
            origin = (((x_at - kx) & 3) * 8 + ((z_at - kz) & 7)) * 2
            pieces[origin + core] = same_core[kx, kz]
            pieces[origin + 1 - core] = other_core[kx, kz]
    h = table[...]

    def target_tile(t):
        return quarters[t]

    to_real(target_tile, target, table, expand, scr_a)

    for k in range(SRC):

        def source_tile(t):
            return pieces[t, k]

        to_real(source_tile, source, table, expand, scr_a)

        def density_body(i, _):
            for p in range(4):
                x = i * 8 + 2 * p
                dens = jnp.concatenate(
                    [target[x] * source[x], target[x + 1] * source[x + 1]], axis=1
                )
                put(scr_a, x, dot(dot(h, dens).astype(BF), twin[...]))
            return 0

        lax.fori_loop(0, 10, density_body, 0)

        def filter_body(i, _):
            for p in range(4):
                y = i * 8 + 2 * p
                spec = dot(h, turned(scr_a, y))
                y0 = jnp.minimum(y, N - y)
                y1 = jnp.minimum(y + 1, N - 1 - y)
                weight = jnp.concatenate([screen[y0], screen[y1]], axis=1)
                put(scr_b, y, dot(h, (spec * weight).astype(BF)))
            return 0

        lax.fori_loop(0, 10, filter_body, 0)

        def potential_body(i, _):
            for p in range(4):
                x = i * 8 + 2 * p
                pot = dot(h, dot(turned(scr_b, x), twin[...]).astype(BF))
                for e in range(2):
                    term = source[x + e].astype(F32) * pot[:, e * LANES : (e + 1) * LANES]
                    if k == 0:
                        partial[x + e] = term
                    else:
                        partial[x + e] = partial[x + e] + term
            return 0

        lax.fori_loop(0, 10, potential_body, 0)

    def last_y_body(i, _):
        for p in range(4):
            x = i * 8 + 2 * p
            both = jnp.concatenate([partial[x].astype(BF), partial[x + 1].astype(BF)], axis=1)
            put(scr_a, x, dot(h, both))
        return 0

    lax.fori_loop(0, 10, last_y_body, 0)

    def last_z_body(i, _):
        y = i * 8
        eight = jnp.concatenate([turned(scr_a, y + 2 * p) for p in range(4)], axis=1)
        r0 = dot(eight[:, :512], c0[...]).astype(BF)
        r1 = dot(eight[:, 384:896], c1[...]).astype(BF)
        r2 = dot(eight[:, 768:], c2[...]).astype(BF)
        t = i * 5
        final[t] = r0[:, :LANES]
        final[t + 1] = r0[:, LANES:]
        final[t + 2] = r1[:, :LANES]
        final[t + 3] = r1[:, LANES:]
        final[t + 4] = r2
        return 0

    lax.fori_loop(0, 10, last_z_body, 0)
    final[TILES] = jnp.zeros((N, LANES), BF)
    final[TILES + 1] = jnp.zeros((N, LANES), BF)
    for k, out in enumerate((out0, out1, out2, out3)):
        start = ((g + k) & 3) * QUART
        for t in range(QUART):
            out[t] = final[start + t]


def select_kernel(own, got1, got2, got3, sel_t, msg, scr):
    tables = [sel_t[c] for c in range(SLOTS)]
    for t in range(QUART):
        total = (
            own[t].astype(F32) + got1[t].astype(F32) + got2[t].astype(F32) + got3[t].astype(F32)
        ).astype(BF)
        for c in range(SLOTS):
            scr[(c * QUART + t) * BANDS : (c * QUART + t + 1) * BANDS, :] = dot(tables[c], total)

    def body(d, _):
        msg[d] = scr[pl.ds(d, ROWS_T, stride=BANDS), :].astype(BF)
        return 0

    lax.fori_loop(0, BANDS, body, 0, unroll=8)


def rows_out_kernel(got, out, scr):
    def load(b, _):
        scr[pl.ds(pl.multiple_of(b * ROWS_T, 8), ROWS_T), :] = got[b].astype(F32)
        return 0

    lax.fori_loop(0, BANDS, load, 0, unroll=8)
    for c in range(SLOTS):
        for t in range(QUART):
            out[c, :, t * LANES : (t + 1) * LANES] = scr[
                pl.ds(c * QUART + t, BANDS, stride=ROWS_T), :
            ].astype(BF)


def join_kernel(own, got1, got2, got3, out):
    g = lax.axis_index("grp")
    wide = QUART * LANES
    short = (TILES - 3 * QUART) * LANES
    for k, ref in enumerate((own, got1, got2, got3)):
        origin = (g - k) & 3
        start = pl.multiple_of(origin * wide, LANES)

        @pl.when(origin < 3)
        def _():
            for c in range(SLOTS):
                out[c, :, pl.ds(start, wide)] = ref[c]

        @pl.when(origin == 3)
        def _():
            for c in range(SLOTS):
                out[c, :, 3 * wide :] = ref[c, :, :short]


VM = pl.BlockSpec(memory_space=pltpu.VMEM)
SM = pl.BlockSpec(memory_space=pltpu.SMEM)
ANY = pl.BlockSpec(memory_space=pl.ANY)
PARAMS = pltpu.CompilerParams(vmem_limit_bytes=56 * 1024 * 1024)


def shape(dims, kind=BF):
    return jax.ShapeDtypeStruct(dims, kind)


def shift_grp(value, k):
    return lax.ppermute(value, "grp", [(i, (i + k) % GROUPS) for i in range(GROUPS)])


def shift_band(value, dx, dz, dc):
    moves = []
    for x in range(4):
        for z in range(8):
            for c in range(2):
                there = (((x + dx) % 4) * 8 + (z + dz) % 8) * 2 + (c + dc) % 2
                moves.append(((x * 8 + z) * 2 + c, there))
    return lax.ppermute(value, "band", moves)


def shards(stick_data, row_lengths, row_order, source_order):
    table = jnp.asarray(hartley_table())
    expand = jnp.asarray(expand_tables(hartley_table()))
    twin = jnp.asarray(pair_table(hartley_table()))
    c0, c1, c2 = (jnp.asarray(v) for v in compress_tables(hartley_table()))
    screen = jnp.asarray(screen_table())

    msg_t, msg_s, sel, sel_t = pl.pallas_call(
        pack_kernel,
        out_shape=(
            shape((BANDS, ROWS_T, LANES)),
            shape((BANDS, ROWS_S, LANES)),
            shape((SLOTS, N, BANDS)),
            shape((SLOTS, BANDS, N)),
        ),
        in_specs=[SM, VM, VM, VM, VM],
        out_specs=(VM, VM, VM, VM),
        scratch_shapes=[
            pltpu.VMEM((ROWS_T * BANDS, LANES), F32),
            pltpu.VMEM((TILES * ROWS_S, LANES), F32),
        ],
        compiler_params=PARAMS,
    )(source_order, stick_data, row_lengths.reshape(1, BANDS), row_order.reshape(1, N), table)

    got_s = lax.all_to_all(msg_s, "band", 0, 0, tiled=True)
    got_t = lax.all_to_all(msg_t, "band", 0, 0, tiled=True)

    quarter, piece = pl.pallas_call(
        rows_kernel,
        out_shape=(shape((QUART, N, LANES)), shape((SRC, N, LANES))),
        in_specs=[VM, VM, VM],
        out_specs=(VM, VM),
        scratch_shapes=[
            pltpu.VMEM((ROWS_T * BANDS, LANES), F32),
            pltpu.VMEM((ROWS_S * BANDS, LANES), F32),
        ],
        compiler_params=PARAMS,
    )(got_t, got_s, sel)

    quarters = lax.all_gather(quarter, "grp", axis=0, tiled=True)
    along_z = jnp.stack([piece] + [shift_band(piece, 0, k, 0) for k in range(1, 8)])
    along_x = jnp.stack([along_z] + [shift_band(along_z, k, 0, 0) for k in range(1, 4)])
    twins = shift_band(along_x, 0, 0, 1)

    outs = pl.pallas_call(
        pairs_kernel,
        out_shape=tuple(shape((QUART, N, LANES)) for _ in range(4)),
        in_specs=[VM] * 10,
        out_specs=(VM,) * 4,
        scratch_shapes=[
            pltpu.VMEM((N, N, LANES), BF),
            pltpu.VMEM((N, N, LANES), BF),
            pltpu.VMEM((N, N, LANES), F32),
            pltpu.VMEM((N * PITCH, LANES), F32),
            pltpu.VMEM((N * PITCH, LANES), F32),
            pltpu.VMEM((TILES + 2, N, LANES), BF),
            pltpu.VMEM((BANDS, SRC, N, LANES), BF),
        ],
        compiler_params=PARAMS,
    )(quarters, along_x, twins, table, expand, twin, c0, c1, c2, screen)

    parts = [outs[0]] + [shift_grp(outs[k], k) for k in range(1, 4)]
    message = pl.pallas_call(
        select_kernel,
        out_shape=shape((BANDS, ROWS_T, LANES)),
        in_specs=[VM] * 5,
        out_specs=VM,
        scratch_shapes=[pltpu.VMEM((ROWS_T * BANDS, LANES), F32)],
        compiler_params=PARAMS,
    )(*parts, sel_t)

    received = lax.all_to_all(message, "band", 0, 0, tiled=True)
    rows = pl.pallas_call(
        rows_out_kernel,
        out_shape=shape((SLOTS, BANDS, QUART * LANES)),
        in_specs=[VM],
        out_specs=VM,
        scratch_shapes=[pltpu.VMEM((ROWS_T * BANDS, LANES), F32)],
        compiler_params=PARAMS,
    )(received)

    others = [shift_grp(rows, k) for k in range(1, 4)]
    return pl.pallas_call(
        join_kernel,
        out_shape=shape((SLOTS, BANDS, TILES * LANES)),
        in_specs=[VM] * 4,
        out_specs=VM,
        compiler_params=PARAMS,
    )(rows, *others)


def solution(mesh):
    return jax.shard_map(
        shards,
        mesh=mesh,
        in_specs=(P("band", None, None), P(), P(), P()),
        out_specs=P("band", None, None),
        check_vma=False,
    )
```

time: 623 us -> 344 us (0.55); the launches traced: 615 us -> 343 us
  waiting for transfers between devices: 315 us -> 112 us
  Pallas kernels: 0 us -> 107 us
  local copies, waits for them, and re-layouts: 108 us -> 2.6 us
  matrix products: 65.3 us -> 0 us
  other arithmetic: 25.6 us -> 0.33 us
  starting transfers between devices: 13.2 us -> 25.3 us
  blocking collectives: 71.3 us -> 83 us
    psum x2 -> x0, waiting for transfers between devices: 247 us -> none  [the longest x1 197 us: broadcast(): return lax.psum(block, axis)]
    pallas_call x0 -> x6, Pallas kernels: none -> 107 us  [the longest x1 91.1 us: shards(): pl.pallas_call(pairs_kernel, out_shape=tuple((shape((QUART, N, LANES)) fo...]
    ppermute x0 -> x17, waiting for transfers between devices: none -> 87.7 us  [the longest x11 45.5 us: shift_band(): return lax.ppermute(value, 'band', moves)]
    another operation x18 -> x1, local copies, waits for them, and re-layouts: 78.9 us -> 0.02 us  [shards(): jnp.stack([piece] + [shift_band(piece, 0, k, 0) for k in range(1, 8)])]
    all_to_all x1 -> x0, waiting for transfers between devices: 68 us -> none  [shards(): lax.all_to_all(stick_data, 'band', split_axis=1, concat_axis=0, tiled=True)]
    dot_general x22 -> x0, matrix products: 65.3 us -> none  [the longest x10 27.9 us: transform(): jnp.einsum('kx,bxyz->bkyz', table_x, values, preferred_element_type=jnp.f...]
    ppermute x0 -> x17, starting transfers between devices: none -> 25.3 us  [the longest x11 18.3 us: shift_band(): return lax.ppermute(value, 'band', moves)]
    all_gather x0 -> x1, waiting for transfers between devices: none -> 24.5 us  [shards(): quarters = lax.all_gather(quarter, 'grp', axis=0, tiled=True)]
  transfers between devices with their start and end apart: 3 -> 18, of which waited for: 3 -> 13; matrix products, arithmetic and copies ran while one was open for 1% -> 0% of each run, Pallas kernels for 0% -> 0%
where the time goes in v1:
time: 344 us; the launch traced here: 343 us
  waiting for transfers between devices  112 us (33%)
  Pallas kernels  107 us (31%)
  blocking collectives  83 us (24%)
  starting transfers between devices  25.3 us (7%)
  between operations  13.5 us (4%)
    pallas_call x1, Pallas kernels, shards(): pl.pallas_call(pairs_kernel, out_shape=tuple((shape((QUART, N, LANES)) fo...  91.1 us
    ppermute x11, waiting for transfers between devices, shift_band(): return lax.ppermute(value, 'band', moves)  45.5 us
    ppermute x6, waiting for transfers between devices, shift_grp(): lax.ppermute(value, 'grp', [(i, (i + k) % GROUPS) for i in range(GROUPS)])  42.2 us
    all_to_all x1, blocking collectives, shards(): received = lax.all_to_all(message, 'band', 0, 0, tiled=True)  31.7 us
    all_to_all x1, blocking collectives, shards(): got_t = lax.all_to_all(msg_t, 'band', 0, 0, tiled=True)  26.3 us
    all_to_all x1, blocking collectives, shards(): got_s = lax.all_to_all(msg_s, 'band', 0, 0, tiled=True)  25.1 us
    all_gather x1, waiting for transfers between devices, shards(): quarters = lax.all_gather(quarter, 'grp', axis=0, tiled=True)  24.5 us
    ppermute x11, starting transfers between devices, shift_band(): return lax.ppermute(value, 'band', moves)  18.3 us
  transfers between devices with their start and end apart: 18, of which 13 were waited for; matrix products, arithmetic and copies ran while one was open for 0% of the time, Pallas kernels for 0%

profile of v1, /device:TPU:1, one launch (start us, length us, event | category | flops | bytes accessed | tf_op | source)
XLA Modules:
  0.0 343.5 jit_solution(8459215096978740687)
XLA Ops:
  6.5 4.1 %shard_map.109 = (bf16[64,40,128]{2,1,0:T(8,128)(2,1)}, bf16[64,16,128]{2,1,0:T(8,128)(2,1)}, bf16[3,80,64]{2,1,0:T(8,128)(2,1)}, bf16[3,64,80]{2,1,0:T(8,128)(2,1)}) custom-call(s32[64]{0:T(128)} %order_s.1, bf16[3,64,6400]{2,1,0:T(8,128)(2,1)} %stick.1, s32[1,64]{1,0:T(1,128)} %bitcast.26, s32[1,80]{1,0:T(1,128)} %bitcast.27, ...), custom_call_target="tpu_custom_call" | custom-call | tf_op jit(solution)/shard_map/pallas_call | solution.py:362
  10.6 25.1 %all_to_all.15.got_s = bf16[64,16,128]{2,1,0:T(8,128)(2,1)} all-to-all(bf16[64,16,128]{2,1,0:T(8,128)(2,1)} %get-tuple-element.16), channel_id=1, replica_groups=mesh['band'=64,'grp'=4] {'band'}, dimensions={0} | all-to-all | bytes 524288 | tf_op jit(solution)/shard_map/all_to_all | solution.py:379
  35.7 26.3 %all_to_all.16.got_t = bf16[64,40,128]{2,1,0:T(8,128)(2,1)} all-to-all(bf16[64,40,128]{2,1,0:T(8,128)(2,1)} %get-tuple-element.15), channel_id=1, replica_groups=mesh['band'=64,'grp'=4] {'band'}, dimensions={0} | all-to-all | bytes 1310720 | tf_op jit(solution)/shard_map/all_to_all | solution.py:380
  61.9 2.6 shard_map.110
  65.1 2.2 collective-permute-start.5
  67.3 2.2 collective-permute-start.4
  69.5 2.0 collective-permute-start.3
  71.9 0.9 bitcast_dynamic-update-slice_fusion.7
  72.8 4.3 %collective-permute-done = bf16[4,80,128]{2,1,0:T(8,128)(2,1)S(1)} collective-permute-done((bf16[4,80,128]{2,1,0:T(8,128)(2,1)}, bf16[4,80,128]{2,1,0:T(8,128)(2,1)S(1)}, u32[]{:S(2)}, u32[]{:S(2)}) %collective-permute-start) | collective-permute-done | bytes 81952 | tf_op jit(solution)/shard_map/ppermute | solution.py:352
  77.7 6.2 %collective-permute-done.1 = bf16[4,80,128]{2,1,0:T(8,128)(2,1)S(1)} collective-permute-done((bf16[4,80,128]{2,1,0:T(8,128)(2,1)}, bf16[4,80,128]{2,1,0:T(8,128)(2,1)S(1)}, u32[]{:S(2)}, u32[]{:S(2)}) %collective-permute-start.1) | collective-permute-done | bytes 81952 | tf_op jit(solution)/shard_map/ppermute | solution.py:352
  84.5 5.8 %collective-permute-done.2 = bf16[4,80,128]{2,1,0:T(8,128)(2,1)S(1)} collective-permute-done((bf16[4,80,128]{2,1,0:T(8,128)(2,1)}, bf16[4,80,128]{2,1,0:T(8,128)(2,1)S(1)}, u32[]{:S(2)}, u32[]{:S(2)}) %collective-permute-start.2) | collective-permute-done | bytes 81952 | tf_op jit(solution)/shard_map/ppermute | solution.py:352
  90.5 3.3 collective-permute-start.9
  93.8 5.8 %collective-permute-start.8 = (bf16[8,4,80,128]{3,2,1,0:T(8,128)(2,1)S(1)}, bf16[8,4,80,128]{3,2,1,0:T(8,128)(2,1)S(1)}, u32[]{:S(2)}, u32[]{:S(2)}) collective-permute-start(bf16[8,4,80,128]{3,2,1,0:T(8,128)(2,1)S(1)} %bitcast_dynamic-update-slice_fusion), channel_id=1, source_target_pairs={{0,128},{4,132},{8,136},{12,140},{16,144},{20,148},{24,152},{28,15... | collective-permute-start | bytes 1966088 | tf_op jit(solution)/shard_map/ppermute | solution.py:352
  99.5 12.7 %collective-permute-done.9 = bf16[8,4,80,128]{3,2,1,0:T(8,128)(2,1)S(1)} collective-permute-done((bf16[8,4,80,128]{3,2,1,0:T(8,128)(2,1)S(1)}, bf16[8,4,80,128]{3,2,1,0:T(8,128)(2,1)S(1)}, u32[]{:S(2)}, u32[]{:S(2)}) %collective-permute-start.9) | collective-permute-done | bytes 655392 | tf_op jit(solution)/shard_map/ppermute | solution.py:352
  112.8 16.0 %collective-permute-done.7 = bf16[8,4,80,128]{3,2,1,0:T(8,128)(2,1)S(1)} collective-permute-done((bf16[8,4,80,128]{3,2,1,0:T(8,128)(2,1)S(1)}, bf16[8,4,80,128]{3,2,1,0:T(8,128)(2,1)S(1)}, u32[]{:S(2)}, u32[]{:S(2)}) %collective-permute-start.7) | collective-permute-done | bytes 655392 | tf_op jit(solution)/shard_map/ppermute | solution.py:352
  129.1 0.8 collective-permute-start.10
  129.9 24.5 %all-gather.2.cloned.1.call-done.quarters = bf16[52,80,128]{2,1,0:T(8,128)(2,1)} async-done(((bf16[13,80,128]{2,1,0:T(8,128)(2,1)}), bf16[52,80,128]{2,1,0:T(8,128)(2,1)}) %all-gather.2.cloned.1.call-update) | async-done | bytes 1064976 | tf_op jit(solution)/shard_map/all_gather | solution.py:394
  154.4 91.1 %shard_map.111 = (bf16[13,80,128]{2,1,0:T(8,128)(2,1)}, bf16[13,80,128]{2,1,0:T(8,128)(2,1)}, bf16[13,80,128]{2,1,0:T(8,128)(2,1)}, bf16[13,80,128]{2,1,0:T(8,128)(2,1)}) custom-call(bf16[52,80,128]{2,1,0:T(8,128)(2,1)} %all-gather.2.cloned.1.call-done.quarters, bf16[4,8,4,80,128]{4,3,2,1,0:T(8,128)(2,1)} %copy-done, ...), custom_call_target="tpu_custom_call" | custom-call | tf_op jit(solution)/shard_map/pallas_call | solution.py:399
  245.5 2.4 collective-permute-start.12
  247.9 1.5 collective-permute-start.13
  249.4 4.2 %collective-permute-done.11.got1 = bf16[13,80,128]{2,1,0:T(8,128)(2,1)S(1)} collective-permute-done((bf16[13,80,128]{2,1,0:T(8,128)(2,1)}, bf16[13,80,128]{2,1,0:T(8,128)(2,1)S(1)}, u32[]{:S(2)}, u32[]{:S(2)}) %collective-permute-start.11) | collective-permute-done | bytes 266272 | tf_op jit(solution)/shard_map/ppermute | solution.py:342
  253.5 5.0 %collective-permute-done.12.got2 = bf16[13,80,128]{2,1,0:T(8,128)(2,1)S(1)} collective-permute-done((bf16[13,80,128]{2,1,0:T(8,128)(2,1)}, bf16[13,80,128]{2,1,0:T(8,128)(2,1)S(1)}, u32[]{:S(2)}, u32[]{:S(2)}) %collective-permute-start.12) | collective-permute-done | bytes 266272 | tf_op jit(solution)/shard_map/ppermute | solution.py:342
  258.6 2.0 collective-permute-done.13.got3
  261.3 3.2 shard_map.112
  264.5 31.7 %all_to_all.17.got = bf16[64,40,128]{2,1,0:T(8,128)(2,1)} all-to-all(bf16[64,40,128]{2,1,0:T(8,128)(2,1)} %shard_map.112), channel_id=1, replica_groups=mesh['band'=64,'grp'=4] {'band'}, dimensions={0} | all-to-all | bytes 1310720 | tf_op jit(solution)/shard_map/all_to_all | solution.py:426
  296.1 2.3 shard_map.113.own
  298.4 2.3 collective-permute-start.16
  301.4 13.7 %collective-permute-done.16.got3 = bf16[3,64,1664]{2,1,0:T(8,128)(2,1)S(1)} collective-permute-done((bf16[3,64,1664]{2,1,0:T(8,128)(2,1)}, bf16[3,64,1664]{2,1,0:T(8,128)(2,1)S(1)}, u32[]{:S(2)}, u32[]{:S(2)}) %collective-permute-start.16) | collective-permute-done | bytes 639008 | tf_op jit(solution)/shard_map/ppermute | solution.py:342
  315.2 2.7 collective-permute-done.15.got2
  317.9 14.6 %collective-permute-done.14.got1 = bf16[3,64,1664]{2,1,0:T(8,128)(2,1)S(1)} collective-permute-done((bf16[3,64,1664]{2,1,0:T(8,128)(2,1)}, bf16[3,64,1664]{2,1,0:T(8,128)(2,1)S(1)}, u32[]{:S(2)}, u32[]{:S(2)}) %collective-permute-start.14) | collective-permute-done | bytes 639008 | tf_op jit(solution)/shard_map/ppermute | solution.py:342
  332.5 0.8 copy-done.3
  333.3 3.3 shard_map.114
  (37 shorter events, 4.5 us)
Async XLA Ops:
  6.5 147.8 %all-gather.2.cloned.1.call-start = ((), (), s32[]{:S(2)}) async-start(), calls=%async_computation.3 | async-start | bytes 1331200 | tf_op jit(solution)/shard_map/all_gather | solution.py:394
  64.6 25.9 %collective-permute-start.6 = (bf16[4,80,128]{2,1,0:T(8,128)(2,1)}, bf16[4,80,128]{2,1,0:T(8,128)(2,1)S(1)}, u32[]{:S(2)}, u32[]{:S(2)}) collective-permute-start(bf16[4,80,128]{2,1,0:T(8,128)(2,1)} %get-tuple-element.19), channel_id=1, source_target_pairs={{0,56},{4,60},{8,0},{12,4},{16,8},{20,12},{24,16},{28,20},{32,24},... | collective-permute-start | bytes 245768 | tf_op jit(solution)/shard_map/ppermute | solution.py:352
  65.1 25.4 %collective-permute-start.5 = (bf16[4,80,128]{2,1,0:T(8,128)(2,1)}, bf16[4,80,128]{2,1,0:T(8,128)(2,1)S(1)}, u32[]{:S(2)}, u32[]{:S(2)}) collective-permute-start(bf16[4,80,128]{2,1,0:T(8,128)(2,1)} %get-tuple-element.19), channel_id=1, source_target_pairs={{0,48},{4,52},{8,56},{12,60},{16,0},{20,4},{24,8},{28,12},{32,16},... | collective-permute-start | bytes 245768 | tf_op jit(solution)/shard_map/ppermute | solution.py:352
  67.3 23.1 %collective-permute-start.4 = (bf16[4,80,128]{2,1,0:T(8,128)(2,1)}, bf16[4,80,128]{2,1,0:T(8,128)(2,1)S(1)}, u32[]{:S(2)}, u32[]{:S(2)}) collective-permute-start(bf16[4,80,128]{2,1,0:T(8,128)(2,1)} %get-tuple-element.19), channel_id=1, source_target_pairs={{0,40},{4,44},{8,48},{12,52},{16,56},{20,60},{24,0},{28,4},{32,8},... | collective-permute-start | bytes 245768 | tf_op jit(solution)/shard_map/ppermute | solution.py:352
  69.5 20.9 %collective-permute-start.3 = (bf16[4,80,128]{2,1,0:T(8,128)(2,1)}, bf16[4,80,128]{2,1,0:T(8,128)(2,1)S(1)}, u32[]{:S(2)}, u32[]{:S(2)}) collective-permute-start(bf16[4,80,128]{2,1,0:T(8,128)(2,1)} %get-tuple-element.19), channel_id=1, source_target_pairs={{0,32},{4,36},{8,40},{12,44},{16,48},{20,52},{24,56},{28,60},{32,0... | collective-permute-start | bytes 245768 | tf_op jit(solution)/shard_map/ppermute | solution.py:352
  71.5 5.6 %collective-permute-start = (bf16[4,80,128]{2,1,0:T(8,128)(2,1)}, bf16[4,80,128]{2,1,0:T(8,128)(2,1)S(1)}, u32[]{:S(2)}, u32[]{:S(2)}) collective-permute-start(bf16[4,80,128]{2,1,0:T(8,128)(2,1)} %get-tuple-element.19), channel_id=1, source_target_pairs={{0,8},{4,12},{8,16},{12,20},{16,24},{20,28},{24,32},{28,36},{32,40... | collective-permute-start | bytes 245768 | tf_op jit(solution)/shard_map/ppermute | solution.py:352
  77.1 6.7 %collective-permute-start.1 = (bf16[4,80,128]{2,1,0:T(8,128)(2,1)}, bf16[4,80,128]{2,1,0:T(8,128)(2,1)S(1)}, u32[]{:S(2)}, u32[]{:S(2)}) collective-permute-start(bf16[4,80,128]{2,1,0:T(8,128)(2,1)} %get-tuple-element.19), channel_id=1, source_target_pairs={{0,16},{4,20},{8,24},{12,28},{16,32},{20,36},{24,40},{28,44},{32,4... | collective-permute-start | bytes 245768 | tf_op jit(solution)/shard_map/ppermute | solution.py:352
  83.8 6.6 %collective-permute-start.2 = (bf16[4,80,128]{2,1,0:T(8,128)(2,1)}, bf16[4,80,128]{2,1,0:T(8,128)(2,1)S(1)}, u32[]{:S(2)}, u32[]{:S(2)}) collective-permute-start(bf16[4,80,128]{2,1,0:T(8,128)(2,1)} %get-tuple-element.19), channel_id=1, source_target_pairs={{0,24},{4,28},{8,32},{12,36},{16,40},{20,44},{24,48},{28,52},{32,5... | collective-permute-start | bytes 245768 | tf_op jit(solution)/shard_map/ppermute | solution.py:352
  90.5 21.8 %collective-permute-start.9 = (bf16[8,4,80,128]{3,2,1,0:T(8,128)(2,1)S(1)}, bf16[8,4,80,128]{3,2,1,0:T(8,128)(2,1)S(1)}, u32[]{:S(2)}, u32[]{:S(2)}) collective-permute-start(bf16[8,4,80,128]{3,2,1,0:T(8,128)(2,1)S(1)} %bitcast_dynamic-update-slice_fusion), channel_id=1, source_target_pairs={{0,192},{4,196},{8,200},{12,204},{16,208},{20,212},{24,216},{28,22... | collective-permute-start | bytes 1966088 | tf_op jit(solution)/shard_map/ppermute | solution.py:352
  93.8 19.0 %collective-permute-start.8 = (bf16[8,4,80,128]{3,2,1,0:T(8,128)(2,1)S(1)}, bf16[8,4,80,128]{3,2,1,0:T(8,128)(2,1)S(1)}, u32[]{:S(2)}, u32[]{:S(2)}) collective-permute-start(bf16[8,4,80,128]{3,2,1,0:T(8,128)(2,1)S(1)} %bitcast_dynamic-update-slice_fusion), channel_id=1, source_target_pairs={{0,128},{4,132},{8,136},{12,140},{16,144},{20,148},{24,152},{28,15... | collective-permute-start | bytes 1966088 | tf_op jit(solution)/shard_map/ppermute | solution.py:352
  99.5 29.2 %collective-permute-start.7 = (bf16[8,4,80,128]{3,2,1,0:T(8,128)(2,1)S(1)}, bf16[8,4,80,128]{3,2,1,0:T(8,128)(2,1)S(1)}, u32[]{:S(2)}, u32[]{:S(2)}) collective-permute-start(bf16[8,4,80,128]{3,2,1,0:T(8,128)(2,1)S(1)} %bitcast_dynamic-update-slice_fusion), channel_id=1, source_target_pairs={{0,64},{4,68},{8,72},{12,76},{16,80},{20,84},{24,88},{28,92},{32,9... | collective-permute-start | bytes 1966088 | tf_op jit(solution)/shard_map/ppermute | solution.py:352
  129.1 25.3 %copy-start = (bf16[4,8,4,80,128]{4,3,2,1,0:T(8,128)(2,1)}, bf16[4,8,4,80,128]{4,3,2,1,0:T(8,128)(2,1)S(1)}, u32[]{:S(2)}) copy-start(bf16[4,8,4,80,128]{4,3,2,1,0:T(8,128)(2,1)S(1)} %pad_maximum_fusion.same_core) | copy-start | bytes 7864324
  129.1 25.3 %collective-permute-start.10 = (bf16[4,8,4,80,128]{4,3,2,1,0:T(8,128)(2,1)S(1)}, bf16[4,8,4,80,128]{4,3,2,1,0:T(8,128)(2,1)}, u32[]{:S(2)}, u32[]{:S(2)}) collective-permute-start(bf16[4,8,4,80,128]{4,3,2,1,0:T(8,128)(2,1)S(1)} %pad_maximum_fusion.same_core), channel_id=1, source_target_pairs={{0,4},{4,0},{8,12},{12,8},{16,20},{20,16},{24,28},{28,24},{32,36},... | collective-permute-start | bytes 7864328 | tf_op jit(solution)/shard_map/ppermute | solution.py:352
  245.5 8.1 %collective-permute-start.11 = (bf16[13,80,128]{2,1,0:T(8,128)(2,1)}, bf16[13,80,128]{2,1,0:T(8,128)(2,1)S(1)}, u32[]{:S(2)}, u32[]{:S(2)}) collective-permute-start(bf16[13,80,128]{2,1,0:T(8,128)(2,1)} %get-tuple-element.21), channel_id=1, source_target_pairs={{0,1},{1,2},{2,3},{3,0},{4,5},{5,6},{6,7},{7,4},{8,9},{9,10},{10,1... | collective-permute-start | bytes 798728 | tf_op jit(solution)/shard_map/ppermute | solution.py:342
  245.5 13.1 %collective-permute-start.12 = (bf16[13,80,128]{2,1,0:T(8,128)(2,1)}, bf16[13,80,128]{2,1,0:T(8,128)(2,1)S(1)}, u32[]{:S(2)}, u32[]{:S(2)}) collective-permute-start(bf16[13,80,128]{2,1,0:T(8,128)(2,1)} %get-tuple-element.22), channel_id=1, source_target_pairs={{0,2},{1,3},{2,0},{3,1},{4,6},{5,7},{6,4},{7,5},{8,10},{9,11},{10,... | collective-permute-start | bytes 798728 | tf_op jit(solution)/shard_map/ppermute | solution.py:342
  247.9 12.7 %collective-permute-start.13 = (bf16[13,80,128]{2,1,0:T(8,128)(2,1)}, bf16[13,80,128]{2,1,0:T(8,128)(2,1)S(1)}, u32[]{:S(2)}, u32[]{:S(2)}) collective-permute-start(bf16[13,80,128]{2,1,0:T(8,128)(2,1)} %get-tuple-element.23), channel_id=1, source_target_pairs={{0,3},{1,0},{2,1},{3,2},{4,7},{5,4},{6,5},{7,6},{8,11},{9,8},{10,9... | collective-permute-start | bytes 798728 | tf_op jit(solution)/shard_map/ppermute | solution.py:342
  253.5 7.0 %copy-start.4 = (bf16[13,80,128]{2,1,0:T(8,128)(2,1)}, bf16[13,80,128]{2,1,0:T(8,128)(2,1)S(1)}, u32[]{:S(2)}) copy-start(bf16[13,80,128]{2,1,0:T(8,128)(2,1)S(1)} %collective-permute-done.11.got1) | copy-start | bytes 798724
  258.6 2.0 copy-start.5
  260.6 0.7 copy-start.6
  298.4 16.7 %collective-permute-start.16 = (bf16[3,64,1664]{2,1,0:T(8,128)(2,1)}, bf16[3,64,1664]{2,1,0:T(8,128)(2,1)S(1)}, u32[]{:S(2)}, u32[]{:S(2)}) collective-permute-start(bf16[3,64,1664]{2,1,0:T(8,128)(2,1)} %shard_map.113.own), channel_id=1, source_target_pairs={{0,3},{1,0},{2,1},{3,2},{4,7},{5,4},{6,5},{7,6},{8,11},{9,8},{10,9... | collective-permute-start | bytes 1916936 | tf_op jit(solution)/shard_map/ppermute | solution.py:342
  300.8 17.1 %collective-permute-start.15 = (bf16[3,64,1664]{2,1,0:T(8,128)(2,1)}, bf16[3,64,1664]{2,1,0:T(8,128)(2,1)S(1)}, u32[]{:S(2)}, u32[]{:S(2)}) collective-permute-start(bf16[3,64,1664]{2,1,0:T(8,128)(2,1)} %shard_map.113.own), channel_id=1, source_target_pairs={{0,2},{1,3},{2,0},{3,1},{4,6},{5,7},{6,4},{7,5},{8,10},{9,11},{10,... | collective-permute-start | bytes 1916936 | tf_op jit(solution)/shard_map/ppermute | solution.py:342
  301.4 31.1 %collective-permute-start.14 = (bf16[3,64,1664]{2,1,0:T(8,128)(2,1)}, bf16[3,64,1664]{2,1,0:T(8,128)(2,1)S(1)}, u32[]{:S(2)}, u32[]{:S(2)}) collective-permute-start(bf16[3,64,1664]{2,1,0:T(8,128)(2,1)} %shard_map.113.own), channel_id=1, source_target_pairs={{0,1},{1,2},{2,3},{3,0},{4,5},{5,6},{6,7},{7,4},{8,9},{9,10},{10,1... | collective-permute-start | bytes 1916936 | tf_op jit(solution)/shard_map/ppermute | solution.py:342
  315.2 17.3 %copy-start.1 = (bf16[3,64,1664]{2,1,0:T(8,128)(2,1)}, bf16[3,64,1664]{2,1,0:T(8,128)(2,1)S(1)}, u32[]{:S(2)}) copy-start(bf16[3,64,1664]{2,1,0:T(8,128)(2,1)S(1)} %collective-permute-done.16.got3) | copy-start | bytes 1916932
  317.9 14.6 %copy-start.2 = (bf16[3,64,1664]{2,1,0:T(8,128)(2,1)}, bf16[3,64,1664]{2,1,0:T(8,128)(2,1)S(1)}, u32[]{:S(2)}) copy-start(bf16[3,64,1664]{2,1,0:T(8,128)(2,1)S(1)} %collective-permute-done.15.got2) | copy-start | bytes 1916932
  332.5 0.8 copy-start.3
Sparse Core Ops, SparseCore 0:
  130.0 24.3 all-gather.1

commit v2 on v1

v2 whole, which is shorter than its diff:
```python
import functools
import math

import jax
import jax.numpy as jnp
import numpy as np
from jax import lax
from jax.experimental import pallas as pl
from jax.experimental.pallas import tpu as pltpu
from jax.sharding import PartitionSpec as P

N = 80
LANES = 128
TILES = 50
QUART = 13
SRC = 4
SLOTS = 3
BANDS = 64
GROUPS = 4
ROWS_T = 40
ROWS_S = 16
ROWS_M = ROWS_T + ROWS_S
HALF = BANDS // 2
PITCH = 88
BF = jnp.bfloat16
F32 = jnp.float32

coulomb_peak = 4.0
screen_square = 64.0


def hartley_table():
    index = np.arange(N)
    angles = (index[:, None] * index[None, :] % N).astype(np.float32) * np.float32(2.0 * math.pi / N)
    return ((np.cos(angles) + np.sin(angles)) / np.float32(math.sqrt(N))).astype(BF)


def expand_tables(table):
    out = np.zeros((4, 256, 256), BF)
    for p in range(4):
        off = 160 * p % LANES
        out[p, off : off + N, :N] = table
        out[p, off + N : off + 2 * N, LANES : LANES + N] = table
    return out


def pair_table(table):
    out = np.zeros((256, 256), BF)
    out[:N, :N] = table
    out[LANES : LANES + N, LANES : LANES + N] = table
    return out


def compress_tables(table):
    whole = np.zeros((1024, 640), BF)
    for y in range(8):
        whole[y * LANES : y * LANES + N, y * N : (y + 1) * N] = table
    return whole[:512, :256].copy(), whole[384:896, 256:512].copy(), whole[768:, 512:].copy()


def screen_table():
    freq = np.minimum(np.arange(N), N - np.arange(N)).astype(np.float32)
    sq = freq * freq
    total = sq[:41, None, None] + sq[None, :, None] + sq[None, None, :]
    out = np.zeros((41, N, LANES), np.float32)
    out[:, :, :N] = np.float32(coulomb_peak) / (np.float32(1.0) + total / np.float32(screen_square))
    return out


def dot(a, b):
    return jnp.dot(a, b, preferred_element_type=F32)


def dot_tn(a, b):
    return lax.dot_general(a, b, (((0,), (0,)), ((), ())), preferred_element_type=F32)


def pack_kernel(order_s, stick, lengths, order_v, table, msg, sel, sel_t, scr, scr_s):
    g = lax.axis_index("grp")
    lens = lengths[...]
    d0 = lax.broadcasted_iota(jnp.int32, (BANDS, BANDS), 0)
    d1 = lax.broadcasted_iota(jnp.int32, (BANDS, BANDS), 1)
    before = jnp.where(d0 < d1, 1.0, 0.0).astype(BF)
    lens8 = jnp.broadcast_to(lens, (8, BANDS)).astype(F32)
    starts = dot(lens8.astype(BF), before)[:1]
    q0 = lax.broadcasted_iota(jnp.int32, (N, N), 0)
    perm = jnp.where(jnp.broadcast_to(order_v[...], (N, N)) == q0, 1.0, 0.0).astype(BF)
    permuted = dot(table[...], perm).astype(BF)
    place = lax.broadcasted_iota(jnp.int32, (N, BANDS), 0).astype(F32)
    for c in range(SLOTS):
        hit = (place == jnp.broadcast_to(starts + c, (N, BANDS))) & (
            jnp.broadcast_to(lens8[:1], (N, BANDS)) > c
        )
        one = jnp.where(hit, 1.0, 0.0).astype(BF)
        sel[c] = dot(permuted, one).astype(BF)
        sel_t[c] = lax.dot_general(
            one, permuted, (((0,), (1,)), ((), ())), preferred_element_type=F32
        ).astype(BF)
    first = QUART * g
    for c in range(SLOTS):

        def body(t, _):
            lane = pl.multiple_of(jnp.minimum(first + t, TILES - 1) * LANES, LANES)
            row = pl.multiple_of((c * QUART + t) * BANDS, BANDS)
            scr[pl.ds(row, BANDS), :] = stick[c, :, pl.ds(lane, LANES)].astype(F32)
            return 0

        lax.fori_loop(0, QUART, body, 0, unroll=True)

    b1 = lax.broadcasted_iota(jnp.int32, (16, BANDS), 1)
    r1 = lax.broadcasted_iota(jnp.int32, (16, BANDS), 0)
    pick = jnp.zeros((16, BANDS), F32)
    for k in range(SRC):
        pick = jnp.where((r1 == k) & (b1 == order_s[g * SRC + k]), 1.0, pick)
    pick = pick.astype(BF)
    for c in range(SLOTS):
        for u in range(TILES // 2):
            got = dot(pick, stick[c, :, u * 256 : u * 256 + 256])
            for h in range(2):
                row = (2 * u + h) * ROWS_S + c * SRC
                scr_s[row : row + SRC, :] = got[:SRC, h * LANES : (h + 1) * LANES]

    def out_body(b, _):
        mine = scr[pl.ds(b, ROWS_T, stride=BANDS), :]
        tile = scr_s[pl.ds(pl.multiple_of(b * ROWS_S, 8), ROWS_S), :]
        msg[b] = jnp.concatenate([mine, tile], axis=0).astype(BF)
        return 0

    lax.fori_loop(0, BANDS, out_body, 0, unroll=8)


def rows_kernel(got, sel, quarter, piece, scr):
    def load(d, _):
        scr[pl.ds(pl.multiple_of(d * ROWS_M, 8), ROWS_M), :] = got[d].astype(F32)
        return 0

    lax.fori_loop(0, BANDS, load, 0, unroll=8)
    tables = [sel[c] for c in range(SLOTS)]
    for out, count, first in ((piece, SRC, ROWS_T), (quarter, QUART, 0)):
        for t in range(count):
            total = jnp.zeros((N, LANES), F32)
            for c in range(SLOTS):
                rows = scr[pl.ds(first + c * count + t, BANDS, stride=ROWS_M), :].astype(BF)
                total = total + dot(tables[c], rows)
            out[t] = total.astype(BF)


def turned(scr, index):
    return jnp.concatenate(
        [
            scr[pl.ds(index, N, stride=PITCH), :].astype(BF),
            scr[pl.ds(index + 1, N, stride=PITCH), :].astype(BF),
        ],
        axis=1,
    )


def put(scr, index, values):
    scr[index * PITCH : index * PITCH + N, :] = values[:, :LANES]
    scr[(index + 1) * PITCH : (index + 1) * PITCH + N, :] = values[:, LANES:]


def side(ref, index):
    return jnp.concatenate([ref[index], ref[index + 1]], axis=1)


CHUNK = 5


def to_real(tile, out, table, expand, scr):
    for p in range(4):
        for lead in range(0, 10, CHUNK):
            rows = []
            for i in range(lead, lead + CHUNK):
                a = i * 5 + (160 * p) // LANES
                rows.append(jnp.concatenate([tile(a), tile(a + 1)], axis=1))
            res = dot(jnp.concatenate(rows, axis=0), expand[p])
            for j in range(CHUNK):
                put(scr, (lead + j) * 8 + 2 * p, res[j * N : (j + 1) * N])
    h = table[...]
    for x in range(0, N, 2):
        res = dot(h, turned(scr, x)).astype(BF)
        out[x] = res[:, :LANES]
        out[x + 1] = res[:, LANES:]


def target_kernel(own, got1, got2, got3, table, expand, out, scr, quarters):
    g = lax.axis_index("grp")
    for k, ref in enumerate((own, got1, got2, got3)):
        start = ((g - k) & 3) * QUART
        for t in range(QUART):
            quarters[start + t] = ref[t]
    to_real(lambda t: quarters[t], out, table, expand, scr)


def gather_tiles(same_core, other_core, pieces):
    band = lax.axis_index("band")
    core, z_at, x_at = band & 1, (band >> 1) & 7, band >> 4
    for kx in range(4):
        for kz in range(8):
            origin = (((x_at - kx) & 3) * 8 + ((z_at - kz) & 7)) * 2
            for e in range(2):
                pieces[origin + core, 2 * e : 2 * e + 2] = same_core[2 * kx + e][kz]
                pieces[origin + 1 - core, 2 * e : 2 * e + 2] = other_core[2 * kx + e][kz]


def one_source(pieces, k, target, source, partial, table, expand, twin, screen, scr_a, scr_b):
    to_real(lambda t: pieces[t, k], source, table, expand, scr_a)
    h = table[...]
    turn = twin[...]
    for lead in range(0, N, 2 * CHUNK):
        rows = []
        for x in range(lead, lead + 2 * CHUNK, 2):
            rows.append(dot(h, side(target, x) * side(source, x)).astype(BF))
        res = dot(jnp.concatenate(rows, axis=0), turn)
        for j in range(CHUNK):
            put(scr_a, lead + 2 * j, res[j * N : (j + 1) * N])
    for y in range(0, N, 2):
        spec = dot(h, turned(scr_a, y))
        weight = jnp.concatenate([screen[min(y, N - y)], screen[min(y + 1, N - 1 - y)]], axis=1)
        put(scr_b, y, dot(h, (spec * weight).astype(BF)))
    for lead in range(0, N, 2 * CHUNK):
        rows = [turned(scr_b, x) for x in range(lead, lead + 2 * CHUNK, 2)]
        res = dot(jnp.concatenate(rows, axis=0), turn).astype(BF)
        for j in range(CHUNK):
            pot = dot(h, res[j * N : (j + 1) * N])
            for e in range(2):
                x = lead + 2 * j + e
                term = source[x].astype(F32) * pot[:, e * LANES : (e + 1) * LANES]
                partial[x] = partial[x] + term


def last_transform(partial, table, c0, c1, c2, scr, final):
    h = table[...]
    for x in range(0, N, 2):
        put(scr, x, dot(h, side(partial, x).astype(BF)))
    blocks = [[turned(scr, y + 2 * p) for p in range(4)] for y in range(0, N, 8)]
    for i in range(0, 10, CHUNK):
        eights = [jnp.concatenate(blocks[i + j], axis=1) for j in range(CHUNK)]
        r0 = dot(jnp.concatenate([v[:, :512] for v in eights], axis=0), c0[...]).astype(BF)
        r1 = dot(jnp.concatenate([v[:, 384:896] for v in eights], axis=0), c1[...]).astype(BF)
        r2 = dot(jnp.concatenate([v[:, 768:] for v in eights], axis=0), c2[...]).astype(BF)
        for j in range(CHUNK):
            t = (i + j) * 5
            rows = slice(j * N, (j + 1) * N)
            final[t] = r0[rows, :LANES]
            final[t + 1] = r0[rows, LANES:]
            final[t + 2] = r1[rows, :LANES]
            final[t + 3] = r1[rows, LANES:]
            final[t + 4] = r2[rows]
    final[TILES] = jnp.zeros((N, LANES), BF)
    final[TILES + 1] = jnp.zeros((N, LANES), BF)


def pairs_kernel(*refs):
    same_core, other_core = refs[:8], refs[8:16]
    target, table, expand, twin, c0, c1, c2, screen = refs[16:24]
    outs = refs[24:28]
    source, partial, scr_a, scr_b, final, pieces = refs[28:]
    g = lax.axis_index("grp")
    gather_tiles(same_core, other_core, pieces)
    partial[...] = jnp.zeros_like(partial)

    def body(k, _):
        one_source(pieces, k, target, source, partial, table, expand, twin, screen, scr_a, scr_b)
        return 0

    lax.fori_loop(0, SRC, body, 0)
    last_transform(partial, table, c0, c1, c2, scr_a, final)
    for k, out in enumerate(outs):
        start = ((g + k) & 3) * QUART
        for t in range(QUART):
            out[t] = final[start + t]


def select_kernel(own, got1, got2, got3, sel_t, msg, scr):
    tables = [sel_t[c] for c in range(SLOTS)]
    for t in range(QUART):
        total = (
            own[t].astype(F32) + got1[t].astype(F32) + got2[t].astype(F32) + got3[t].astype(F32)
        ).astype(BF)
        for c in range(SLOTS):
            scr[(c * QUART + t) * BANDS : (c * QUART + t + 1) * BANDS, :] = dot(tables[c], total)

    def body(d, _):
        msg[d] = scr[pl.ds(d, ROWS_T, stride=BANDS), :].astype(BF)
        return 0

    lax.fori_loop(0, BANDS, body, 0, unroll=8)


def rows_out_kernel(got, low, high, scr):
    def load(b, _):
        scr[pl.ds(pl.multiple_of(b * ROWS_T, 8), ROWS_T), :] = got[b].astype(F32)
        return 0

    lax.fori_loop(0, BANDS, load, 0, unroll=8)
    for c in range(SLOTS):
        for t in range(QUART):
            rows = scr[pl.ds(c * QUART + t, BANDS, stride=ROWS_T), :].astype(BF)
            low[c, :, t * LANES : (t + 1) * LANES] = rows[:HALF]
            high[c, :, t * LANES : (t + 1) * LANES] = rows[HALF:]


def join_kernel(*refs):
    out = refs[8]
    g = lax.axis_index("grp")
    wide = QUART * LANES
    short = (TILES - 3 * QUART) * LANES
    for k in range(4):
        origin = (g - k) & 3
        start = pl.multiple_of(origin * wide, LANES)

        @pl.when(origin < 3)
        def _():
            for c in range(SLOTS):
                for e in range(2):
                    out[c, e * HALF : (e + 1) * HALF, pl.ds(start, wide)] = refs[2 * k + e][c]

        @pl.when(origin == 3)
        def _():
            for c in range(SLOTS):
                for e in range(2):
                    out[c, e * HALF : (e + 1) * HALF, 3 * wide :] = refs[2 * k + e][c, :, :short]


VM = pl.BlockSpec(memory_space=pltpu.VMEM)
SM = pl.BlockSpec(memory_space=pltpu.SMEM)
ANY = pl.BlockSpec(memory_space=pl.ANY)
PARAMS = pltpu.CompilerParams(vmem_limit_bytes=56 * 1024 * 1024)


def shape(dims, kind=BF):
    return jax.ShapeDtypeStruct(dims, kind)


def shift_grp(value, k):
    return lax.ppermute(value, "grp", [(i, (i + k) % GROUPS) for i in range(GROUPS)])


def shift_band(value, dx, dz, dc):
    moves = []
    for x in range(4):
        for z in range(8):
            for c in range(2):
                there = (((x + dx) % 4) * 8 + (z + dz) % 8) * 2 + (c + dc) % 2
                moves.append(((x * 8 + z) * 2 + c, there))
    return lax.ppermute(value, "band", moves)


def ring_gather(first, second, step):
    ahead = step(first, 1), step(second, 1)
    behind = step(first, 3), step(second, 3)
    far = step(ahead[0], 1), step(behind[1], 3)
    return [(first, second), ahead, far, behind]


def shards(stick_data, row_lengths, row_order, source_order):
    table = jnp.asarray(hartley_table())
    expand = jnp.asarray(expand_tables(hartley_table()))
    twin = jnp.asarray(pair_table(hartley_table()))
    c0, c1, c2 = (jnp.asarray(v) for v in compress_tables(hartley_table()))
    screen = jnp.asarray(screen_table())

    msg, sel, sel_t = pl.pallas_call(
        pack_kernel,
        out_shape=(
            shape((BANDS, ROWS_M, LANES)),
            shape((SLOTS, N, BANDS)),
            shape((SLOTS, BANDS, N)),
        ),
        in_specs=[SM, VM, VM, VM, VM],
        out_specs=(VM, VM, VM),
        scratch_shapes=[
            pltpu.VMEM((ROWS_T * BANDS, LANES), F32),
            pltpu.VMEM((BANDS * ROWS_S, LANES), F32),
        ],
        compiler_params=PARAMS,
    )(source_order, stick_data, row_lengths.reshape(1, BANDS), row_order.reshape(1, N), table)
    got = lax.all_to_all(msg, "band", 0, 0, tiled=True)
    quarter, piece = pl.pallas_call(
        rows_kernel,
        out_shape=(shape((QUART, N, LANES)), shape((SRC, N, LANES))),
        in_specs=[VM, VM],
        out_specs=(VM, VM),
        scratch_shapes=[pltpu.VMEM((ROWS_M * BANDS, LANES), F32)],
        compiler_params=PARAMS,
    )(got, sel)

    along_z = [piece] + [shift_band(piece, 0, k, 0) for k in range(1, 8)]
    quarters = [quarter] + [shift_grp(quarter, k) for k in range(1, 4)]
    halves = [jnp.stack([v[2 * e : 2 * e + 2] for v in along_z]) for e in range(2)]
    gathered = ring_gather(*halves, lambda v, k: shift_band(v, k, 0, 0))
    same_core = [v for both in gathered for v in both]
    other_core = [shift_band(v, 0, 0, 1) for v in same_core]

    target = pl.pallas_call(
        target_kernel,
        out_shape=shape((N, N, LANES)),
        in_specs=[VM] * 6,
        out_specs=VM,
        scratch_shapes=[
            pltpu.VMEM((N * PITCH, LANES), F32),
            pltpu.VMEM((4 * QUART, N, LANES), BF),
        ],
        compiler_params=PARAMS,
    )(*quarters, table, expand)

    outs = pl.pallas_call(
        pairs_kernel,
        out_shape=tuple(shape((QUART, N, LANES)) for _ in range(4)),
        in_specs=[VM] * 24,
        out_specs=(VM,) * 4,
        scratch_shapes=[
            pltpu.VMEM((N, N, LANES), BF),
            pltpu.VMEM((N, N, LANES), F32),
            pltpu.VMEM((N * PITCH, LANES), F32),
            pltpu.VMEM((N * PITCH, LANES), F32),
            pltpu.VMEM((TILES + 2, N, LANES), BF),
            pltpu.VMEM((BANDS, SRC, N, LANES), BF),
        ],
        compiler_params=PARAMS,
    )(*same_core, *other_core, target, table, expand, twin, c0, c1, c2, screen)

    parts = [outs[0]] + [shift_grp(outs[k], k) for k in range(1, 4)]
    message = pl.pallas_call(
        select_kernel,
        out_shape=shape((BANDS, ROWS_T, LANES)),
        in_specs=[VM] * 5,
        out_specs=VM,
        scratch_shapes=[pltpu.VMEM((ROWS_T * BANDS, LANES), F32)],
        compiler_params=PARAMS,
    )(*parts, sel_t)

    received = lax.all_to_all(message, "band", 0, 0, tiled=True)
    low, high = pl.pallas_call(
        rows_out_kernel,
        out_shape=(shape((SLOTS, HALF, QUART * LANES)),) * 2,
        in_specs=[VM],
        out_specs=(VM, VM),
        scratch_shapes=[pltpu.VMEM((ROWS_T * BANDS, LANES), F32)],
        compiler_params=PARAMS,
    )(received)

    spread = ring_gather(low, high, shift_grp)
    return pl.pallas_call(
        join_kernel,
        out_shape=shape((SLOTS, BANDS, TILES * LANES)),
        in_specs=[VM] * 8,
        out_specs=VM,
        compiler_params=PARAMS,
    )(*[v for both in spread for v in both])


def solution(mesh):
    return jax.shard_map(
        shards,
        mesh=mesh,
        in_specs=(P("band", None, None), P(), P(), P()),
        out_specs=P("band", None, None),
        check_vma=False,
    )
```

time: 344 us -> 231 us (0.67)
  Pallas kernels: 107 us -> 45.3 us
  waiting for transfers between devices: 112 us -> 65.5 us
  starting transfers between devices: 25.3 us -> 45.1 us
  blocking collectives: 83 us -> 69.5 us
  between operations: 13.5 us -> 0.33 us
    pallas_call x1, Pallas kernels: 91.1 us -> 25.7 us  [shards(): pl.pallas_call(pairs_kernel, out_shape=tuple((shape((QUART, N, LANES)) fo...]
    all_gather x1 -> x0, waiting for transfers between devices: 24.5 us -> none  [shards(): quarters = lax.all_gather(quarter, 'grp', axis=0, tiled=True)]
    ppermute x11 -> x21, waiting for transfers between devices: 45.5 us -> 29.2 us  [shift_band(): return lax.ppermute(value, 'band', moves)]
    ppermute x11 -> x21, starting transfers between devices: 18.3 us -> 31.4 us  [shift_band(): return lax.ppermute(value, 'band', moves)]
    all_to_all x2 -> x1, blocking collectives: 51.4 us -> 38.8 us  [shards(): got = lax.all_to_all(msg, 'band', 0, 0, tiled=True)]
    ppermute x6 -> x12, starting transfers between devices: 6.92 us -> 13.7 us  [shift_grp(): lax.ppermute(value, 'grp', [(i, (i + k) % GROUPS) for i in range(GROUPS)])]
    ppermute x6 -> x12, waiting for transfers between devices: 42.2 us -> 36.3 us  [shift_grp(): lax.ppermute(value, 'grp', [(i, (i + k) % GROUPS) for i in range(GROUPS)])]
    pallas_call x2 -> x3, Pallas kernels: 6.36 us -> 10.4 us  [the longest x1 4.16 us: shards(): pl.pallas_call(pack_kernel, out_shape=(shape((BANDS, ROWS_M, LANES)), sha...]
  transfers between devices with their start and end apart: 18 -> 33, of which waited for: 13 -> 12; matrix products, arithmetic and copies ran while one was open for 0% -> 0% of each run, Pallas kernels for 0% -> 2%
where the time goes in v2:
time: 231 us
  blocking collectives  69.5 us (30%)
  waiting for transfers between devices  65.5 us (28%)
  Pallas kernels  45.3 us (20%)
  starting transfers between devices  45.1 us (20%)
  local copies, waits for them, and re-layouts  4.85 us (2%)
    all_to_all x1, blocking collectives, shards(): got = lax.all_to_all(msg, 'band', 0, 0, tiled=True)  38.8 us
    ppermute x12, waiting for transfers between devices, shift_grp(): lax.ppermute(value, 'grp', [(i, (i + k) % GROUPS) for i in range(GROUPS)])  36.3 us
    ppermute x21, starting transfers between devices, shift_band(): return lax.ppermute(value, 'band', moves)  31.4 us
    all_to_all x1, blocking collectives, shards(): received = lax.all_to_all(message, 'band', 0, 0, tiled=True)  30.6 us
    ppermute x21, waiting for transfers between devices, shift_band(): return lax.ppermute(value, 'band', moves)  29.2 us
    pallas_call x1, Pallas kernels, shards(): pl.pallas_call(pairs_kernel, out_shape=tuple((shape((QUART, N, LANES)) fo...  25.7 us
    ppermute x12, starting transfers between devices, shift_grp(): lax.ppermute(value, 'grp', [(i, (i + k) % GROUPS) for i in range(GROUPS)])  13.7 us
    unnamed x63, local copies, waits for them, and re-layouts  4.84 us
  transfers between devices with their start and end apart: 33, of which 12 were waited for; matrix products, arithmetic and copies ran while one was open for 0% of the time, Pallas kernels for 2%

profile of v2, /device:TPU:1, one launch (start us, length us, event | category | flops | bytes accessed | tf_op | source)
XLA Modules:
  0.0 230.6 jit_solution(12315578382141509837)
XLA Ops:
  0.0 4.2 %shard_map.109 = (bf16[64,56,128]{2,1,0:T(8,128)(2,1)}, bf16[3,80,64]{2,1,0:T(8,128)(2,1)}, bf16[3,64,80]{2,1,0:T(8,128)(2,1)}) custom-call(s32[64]{0:T(128)} %order_s.1, bf16[3,64,6400]{2,1,0:T(8,128)(2,1)} %stick.1, s32[1,64]{1,0:T(1,128)} %bitcast.62, s32[1,80]{1,0:T(1,128)} %bitcast.63, bf16[80,80]{1,0:T(8,128)(2,1)} %constant.14.clone.table.refs_17_), custom_call_target="tpu_custom_call" | custom-call | tf_op jit(solution)/shard_map/pallas_call | solution.py:365
  4.2 38.8 %all_to_all.10.got = bf16[64,56,128]{2,1,0:T(8,128)(2,1)} all-to-all(bf16[64,56,128]{2,1,0:T(8,128)(2,1)} %get-tuple-element.16), channel_id=1, replica_groups=mesh['band'=64,'grp'=4] {'band'}, dimensions={0} | all-to-all | bytes 1835008 | tf_op jit(solution)/shard_map/all_to_all | solution.py:380
  43.0 2.7 %shard_map.110 = (bf16[13,80,128]{2,1,0:T(8,128)(2,1)}, bf16[4,80,128]{2,1,0:T(8,128)(2,1)}) custom-call(bf16[64,56,128]{2,1,0:T(8,128)(2,1)} %all_to_all.10.got, bf16[3,80,64]{2,1,0:T(8,128)(2,1)} %get-tuple-element.17.sel), custom_call_target="tpu_custom_call" | custom-call | tf_op jit(solution)/shard_map/pallas_call | solution.py:381
  46.0 2.4 %collective-permute-start.5 = (bf16[4,80,128]{2,1,0:T(8,128)(2,1)}, bf16[4,80,128]{2,1,0:T(8,128)(2,1)S(1)}, u32[]{:S(2)}, u32[]{:S(2)}) collective-permute-start(bf16[4,80,128]{2,1,0:T(8,128)(2,1)} %get-tuple-element.18), channel_id=1, source_target_pairs={{0,48},{4,52},{8,56},{12,60},{16,0},{20,4},{24,8},{28,12},{32,16},... | collective-permute-start | bytes 245768 | tf_op jit(solution)/shard_map/ppermute | solution.py:348
  48.4 2.0 collective-permute-start.4
  50.3 2.2 collective-permute-start.3
  53.7 4.8 %collective-permute-done = bf16[4,80,128]{2,1,0:T(8,128)(2,1)S(1)} collective-permute-done((bf16[4,80,128]{2,1,0:T(8,128)(2,1)}, bf16[4,80,128]{2,1,0:T(8,128)(2,1)S(1)}, u32[]{:S(2)}, u32[]{:S(2)}) %collective-permute-start) | collective-permute-done | bytes 81952 | tf_op jit(solution)/shard_map/ppermute | solution.py:348
  58.8 5.8 %collective-permute-done.1 = bf16[4,80,128]{2,1,0:T(8,128)(2,1)S(1)} collective-permute-done((bf16[4,80,128]{2,1,0:T(8,128)(2,1)}, bf16[4,80,128]{2,1,0:T(8,128)(2,1)S(1)}, u32[]{:S(2)}, u32[]{:S(2)}) %collective-permute-start.1) | collective-permute-done | bytes 81952 | tf_op jit(solution)/shard_map/ppermute | solution.py:348
  64.9 6.1 %collective-permute-done.2 = bf16[4,80,128]{2,1,0:T(8,128)(2,1)S(1)} collective-permute-done((bf16[4,80,128]{2,1,0:T(8,128)(2,1)}, bf16[4,80,128]{2,1,0:T(8,128)(2,1)S(1)}, u32[]{:S(2)}, u32[]{:S(2)}) %collective-permute-start.2) | collective-permute-done | bytes 81952 | tf_op jit(solution)/shard_map/ppermute | solution.py:348
  71.1 2.7 %collective-permute-start.23 = (bf16[13,80,128]{2,1,0:T(8,128)(2,1)}, bf16[13,80,128]{2,1,0:T(8,128)(2,1)S(1)}, u32[]{:S(2)}, u32[]{:S(2)}) collective-permute-start(bf16[13,80,128]{2,1,0:T(8,128)(2,1)} %get-tuple-element.19.own), channel_id=1, source_target_pairs={{0,3},{1,0},{2,1},{3,2},{4,7},{5,4},{6,5},{7,6},{8,11},{9,8},{10,9... | collective-permute-start | bytes 798728 | tf_op jit(solution)/shard_map/ppermute | solution.py:338
  74.4 6.4 %collective-permute-start.14 = (bf16[8,2,80,128]{3,2,1,0:T(8,128)(2,1)S(1)}, bf16[8,2,80,128]{3,2,1,0:T(8,128)(2,1)S(1)}, u32[]{:S(2)}, u32[]{:S(2)}) collective-permute-start(bf16[8,2,80,128]{3,2,1,0:T(8,128)(2,1)S(1)} %get-tuple-element.27.refs_1_), channel_id=1, source_target_pairs={{0,4},{4,0},{8,12},{12,8},{16,20},{20,16},{24,28},{28,24},{32,36},... | collective-permute-start | bytes 983048 | tf_op jit(solution)/shard_map/ppermute | solution.py:348
  80.8 2.0 collective-permute-start.10
  82.9 1.3 collective-permute-start.7
  84.8 6.9 %collective-permute-done.21.got1 = bf16[13,80,128]{2,1,0:T(8,128)(2,1)S(1)} collective-permute-done((bf16[13,80,128]{2,1,0:T(8,128)(2,1)}, bf16[13,80,128]{2,1,0:T(8,128)(2,1)S(1)}, u32[]{:S(2)}, u32[]{:S(2)}) %collective-permute-start.21) | collective-permute-done | bytes 266272 | tf_op jit(solution)/shard_map/ppermute | solution.py:338
  91.7 6.3 %collective-permute-start.13 = (bf16[8,2,80,128]{3,2,1,0:T(8,128)(2,1)S(1)}, bf16[8,2,80,128]{3,2,1,0:T(8,128)(2,1)S(1)}, u32[]{:S(2)}, u32[]{:S(2)}) collective-permute-start(bf16[8,2,80,128]{3,2,1,0:T(8,128)(2,1)S(1)} %get-tuple-element.28.refs_0_), channel_id=1, source_target_pairs={{0,4},{4,0},{8,12},{12,8},{16,20},{20,16},{24,28},{28,24},{32,36},... | collective-permute-start | bytes 983048 | tf_op jit(solution)/shard_map/ppermute | solution.py:348
  98.9 4.2 %collective-permute-start.11 = (bf16[8,2,80,128]{3,2,1,0:T(8,128)(2,1)S(1)}, bf16[8,2,80,128]{3,2,1,0:T(8,128)(2,1)S(1)}, u32[]{:S(2)}, u32[]{:S(2)}) collective-permute-start(bf16[8,2,80,128]{3,2,1,0:T(8,128)(2,1)S(1)} %collective-permute-done.10.refs_7_), channel_id=1, source_target_pairs={{0,192},{4,196},{8,200},{12,204},{16,208},{20,212},{24,216},{28,22... | collective-permute-start | bytes 983048 | tf_op jit(solution)/shard_map/ppermute | solution.py:348
  103.7 6.5 %collective-permute-done.12.refs_6_ = bf16[8,2,80,128]{3,2,1,0:T(8,128)(2,1)S(1)} collective-permute-done((bf16[8,2,80,128]{3,2,1,0:T(8,128)(2,1)S(1)}, bf16[8,2,80,128]{3,2,1,0:T(8,128)(2,1)S(1)}, u32[]{:S(2)}, u32[]{:S(2)}) %collective-permute-start.12) | collective-permute-done | bytes 327712 | tf_op jit(solution)/shard_map/ppermute | solution.py:348
  111.2 6.0 %collective-permute-done.11.refs_5_ = bf16[8,2,80,128]{3,2,1,0:T(8,128)(2,1)S(1)} collective-permute-done((bf16[8,2,80,128]{3,2,1,0:T(8,128)(2,1)S(1)}, bf16[8,2,80,128]{3,2,1,0:T(8,128)(2,1)S(1)}, u32[]{:S(2)}, u32[]{:S(2)}) %collective-permute-start.11) | collective-permute-done | bytes 327712 | tf_op jit(solution)/shard_map/ppermute | solution.py:348
  118.2 3.9 %shard_map.111.refs_16_ = bf16[80,80,128]{2,1,0:T(8,128)(2,1)} custom-call(bf16[13,80,128]{2,1,0:T(8,128)(2,1)} %get-tuple-element.19.own, bf16[13,80,128]{2,1,0:T(8,128)(2,1)} %copy-done.24, bf16[13,80,128]{2,1,0:T(8,128)(2,1)} %copy-done.23, bf16[13,80,128]{2,1,0:T(8,128)(2,1)} %copy-done.22, bf16[80,80]{1,0:T(8,128)(2,1)} %constant.14.clone.table.refs_17_, ...), custom_call_target="tpu_custom_call" | custom-call | tf_op jit(solution)/shard_map/pallas_call | solution.py:397
  123.9 25.7 %shard_map.112 = (bf16[13,80,128]{2,1,0:T(8,128)(2,1)}, bf16[13,80,128]{2,1,0:T(8,128)(2,1)}, bf16[13,80,128]{2,1,0:T(8,128)(2,1)}, bf16[13,80,128]{2,1,0:T(8,128)(2,1)}) custom-call(bf16[8,2,80,128]{3,2,1,0:T(8,128)(2,1)} %copy-done.1, bf16[8,2,80,128]{3,2,1,0:T(8,128)(2,1)} %copy-done, bf16[8,2,80,128]{3,2,1,0:T(8,128)(2,1)} %copy-done.5, ...), custom_call_target="tpu_custom_call" | custom-call | tf_op jit(solution)/shard_map/pallas_call | solution.py:409
  149.7 3.0 %collective-permute-start.25 = (bf16[13,80,128]{2,1,0:T(8,128)(2,1)}, bf16[13,80,128]{2,1,0:T(8,128)(2,1)S(1)}, u32[]{:S(2)}, u32[]{:S(2)}) collective-permute-start(bf16[13,80,128]{2,1,0:T(8,128)(2,1)} %get-tuple-element.22), channel_id=1, source_target_pairs={{0,2},{1,3},{2,0},{3,1},{4,6},{5,7},{6,4},{7,5},{8,10},{9,11},{10,... | collective-permute-start | bytes 798728 | tf_op jit(solution)/shard_map/ppermute | solution.py:338
  152.7 6.2 %collective-permute-done.24.got1 = bf16[13,80,128]{2,1,0:T(8,128)(2,1)S(1)} collective-permute-done((bf16[13,80,128]{2,1,0:T(8,128)(2,1)}, bf16[13,80,128]{2,1,0:T(8,128)(2,1)S(1)}, u32[]{:S(2)}, u32[]{:S(2)}) %collective-permute-start.24) | collective-permute-done | bytes 266272 | tf_op jit(solution)/shard_map/ppermute | solution.py:338
  158.9 6.0 %collective-permute-done.25.got2 = bf16[13,80,128]{2,1,0:T(8,128)(2,1)S(1)} collective-permute-done((bf16[13,80,128]{2,1,0:T(8,128)(2,1)}, bf16[13,80,128]{2,1,0:T(8,128)(2,1)S(1)}, u32[]{:S(2)}, u32[]{:S(2)}) %collective-permute-start.25) | collective-permute-done | bytes 266272 | tf_op jit(solution)/shard_map/ppermute | solution.py:338
  165.7 3.2 %shard_map.113 = bf16[64,40,128]{2,1,0:T(8,128)(2,1)} custom-call(bf16[13,80,128]{2,1,0:T(8,128)(2,1)} %get-tuple-element.20.own, bf16[13,80,128]{2,1,0:T(8,128)(2,1)} %copy-done.25, bf16[13,80,128]{2,1,0:T(8,128)(2,1)} %copy-done.26, bf16[13,80,128]{2,1,0:T(8,128)(2,1)} %copy-done.27, bf16[3,64,80]{2,1,0:T(8,128)(2,1)} %get-tuple-element.24.sel_t), custom_call_target="tpu_custom_call" | custom-call | tf_op jit(solution)/shard_map/pallas_call | solution.py:426
  168.9 30.6 %all_to_all.11.got = bf16[64,40,128]{2,1,0:T(8,128)(2,1)} all-to-all(bf16[64,40,128]{2,1,0:T(8,128)(2,1)} %shard_map.113), channel_id=1, replica_groups=mesh['band'=64,'grp'=4] {'band'}, dimensions={0} | all-to-all | bytes 1310720 | tf_op jit(solution)/shard_map/all_to_all | solution.py:435
  199.5 2.3 %shard_map.114 = (bf16[3,32,1664]{2,1,0:T(8,128)(2,1)}, bf16[3,32,1664]{2,1,0:T(8,128)(2,1)}) custom-call(bf16[64,40,128]{2,1,0:T(8,128)(2,1)} %all_to_all.11.got), custom_call_target="tpu_custom_call" | custom-call | tf_op jit(solution)/shard_map/pallas_call | solution.py:436
  201.9 2.7 %collective-permute-start.30 = (bf16[3,32,1664]{2,1,0:T(8,128)(2,1)}, bf16[3,32,1664]{2,1,0:T(8,128)(2,1)S(1)}, u32[]{:S(2)}, u32[]{:S(2)}) collective-permute-start(bf16[3,32,1664]{2,1,0:T(8,128)(2,1)} %get-tuple-element.26.refs_1_), channel_id=1, source_target_pairs={{0,3},{1,0},{2,1},{3,2},{4,7},{5,4},{6,5},{7,6},{8,11},{9,8},{10,9... | collective-permute-start | bytes 958472 | tf_op jit(solution)/shard_map/ppermute | solution.py:338
  206.0 6.1 %collective-permute-done.27.refs_2_ = bf16[3,32,1664]{2,1,0:T(8,128)(2,1)S(1)} collective-permute-done((bf16[3,32,1664]{2,1,0:T(8,128)(2,1)}, bf16[3,32,1664]{2,1,0:T(8,128)(2,1)S(1)}, u32[]{:S(2)}, u32[]{:S(2)}) %collective-permute-start.27) | collective-permute-done | bytes 319520 | tf_op jit(solution)/shard_map/ppermute | solution.py:338
  212.1 2.7 %collective-permute-start.31 = (bf16[3,32,1664]{2,1,0:T(8,128)(2,1)S(1)}, bf16[3,32,1664]{2,1,0:T(8,128)(2,1)S(1)}, u32[]{:S(2)}, u32[]{:S(2)}) collective-permute-start(bf16[3,32,1664]{2,1,0:T(8,128)(2,1)S(1)} %collective-permute-done.30.refs_7_), channel_id=1, source_target_pairs={{0,3},{1,0},{2,1},{3,2},{4,7},{5,4},{6,5},{7,6},{8,11},{9,8},{10,9... | collective-permute-start | bytes 958472 | tf_op jit(solution)/shard_map/ppermute | solution.py:338
  214.8 3.2 %collective-permute-done.32.refs_6_ = bf16[3,32,1664]{2,1,0:T(8,128)(2,1)S(1)} collective-permute-done((bf16[3,32,1664]{2,1,0:T(8,128)(2,1)}, bf16[3,32,1664]{2,1,0:T(8,128)(2,1)S(1)}, u32[]{:S(2)}, u32[]{:S(2)}) %collective-permute-start.32) | collective-permute-done | bytes 319520 | tf_op jit(solution)/shard_map/ppermute | solution.py:338
  219.0 6.8 %collective-permute-done.29.refs_4_ = bf16[3,32,1664]{2,1,0:T(8,128)(2,1)S(1)} collective-permute-done((bf16[3,32,1664]{2,1,0:T(8,128)(2,1)S(1)}, bf16[3,32,1664]{2,1,0:T(8,128)(2,1)S(1)}, u32[]{:S(2)}, u32[]{:S(2)}) %collective-permute-start.29) | collective-permute-done | bytes 319520 | tf_op jit(solution)/shard_map/ppermute | solution.py:338
  227.3 3.3 %shard_map.115 = bf16[3,64,6400]{2,1,0:T(8,128)(2,1)} custom-call(bf16[3,32,1664]{2,1,0:T(8,128)(2,1)} %get-tuple-element.25.refs_0_, bf16[3,32,1664]{2,1,0:T(8,128)(2,1)} %get-tuple-element.26.refs_1_, bf16[3,32,1664]{2,1,0:T(8,128)(2,1)} %copy-done.16, bf16[3,32,1664]{2,1,0:T(8,128)(2,1)} %copy-done.19, bf16[3,32,1664]{2,1,0:T(8,128)(2,1)} %copy-done.20, ...), custom_call_target="tpu_custom_call" | custom-call | tf_op jit(solution)/shard_map/pallas_call | solution.py:446
  (107 shorter events, 13.2 us)
Async XLA Ops:
  45.7 28.6 %collective-permute-start.6 = (bf16[4,80,128]{2,1,0:T(8,128)(2,1)}, bf16[4,80,128]{2,1,0:T(8,128)(2,1)S(1)}, u32[]{:S(2)}, u32[]{:S(2)}) collective-permute-start(bf16[4,80,128]{2,1,0:T(8,128)(2,1)} %get-tuple-element.18), channel_id=1, source_target_pairs={{0,56},{4,60},{8,0},{12,4},{16,8},{20,12},{24,16},{28,20},{32,24},... | collective-permute-start | bytes 245768 | tf_op jit(solution)/shard_map/ppermute | solution.py:348
  46.0 28.3 %collective-permute-start.5 = (bf16[4,80,128]{2,1,0:T(8,128)(2,1)}, bf16[4,80,128]{2,1,0:T(8,128)(2,1)S(1)}, u32[]{:S(2)}, u32[]{:S(2)}) collective-permute-start(bf16[4,80,128]{2,1,0:T(8,128)(2,1)} %get-tuple-element.18), channel_id=1, source_target_pairs={{0,48},{4,52},{8,56},{12,60},{16,0},{20,4},{24,8},{28,12},{32,16},... | collective-permute-start | bytes 245768 | tf_op jit(solution)/shard_map/ppermute | solution.py:348
  48.4 25.9 %collective-permute-start.4 = (bf16[4,80,128]{2,1,0:T(8,128)(2,1)}, bf16[4,80,128]{2,1,0:T(8,128)(2,1)S(1)}, u32[]{:S(2)}, u32[]{:S(2)}) collective-permute-start(bf16[4,80,128]{2,1,0:T(8,128)(2,1)} %get-tuple-element.18), channel_id=1, source_target_pairs={{0,40},{4,44},{8,48},{12,52},{16,56},{20,60},{24,0},{28,4},{32,8},... | collective-permute-start | bytes 245768 | tf_op jit(solution)/shard_map/ppermute | solution.py:348
  50.3 23.5 %collective-permute-start.3 = (bf16[4,80,128]{2,1,0:T(8,128)(2,1)}, bf16[4,80,128]{2,1,0:T(8,128)(2,1)S(1)}, u32[]{:S(2)}, u32[]{:S(2)}) collective-permute-start(bf16[4,80,128]{2,1,0:T(8,128)(2,1)} %get-tuple-element.18), channel_id=1, source_target_pairs={{0,32},{4,36},{8,40},{12,44},{16,48},{20,52},{24,56},{28,60},{32,0... | collective-permute-start | bytes 245768 | tf_op jit(solution)/shard_map/ppermute | solution.py:348
  52.6 5.9 %collective-permute-start = (bf16[4,80,128]{2,1,0:T(8,128)(2,1)}, bf16[4,80,128]{2,1,0:T(8,128)(2,1)S(1)}, u32[]{:S(2)}, u32[]{:S(2)}) collective-permute-start(bf16[4,80,128]{2,1,0:T(8,128)(2,1)} %get-tuple-element.18), channel_id=1, source_target_pairs={{0,8},{4,12},{8,16},{12,20},{16,24},{20,28},{24,32},{28,36},{32,40... | collective-permute-start | bytes 245768 | tf_op jit(solution)/shard_map/ppermute | solution.py:348
  58.5 6.0 %collective-permute-start.1 = (bf16[4,80,128]{2,1,0:T(8,128)(2,1)}, bf16[4,80,128]{2,1,0:T(8,128)(2,1)S(1)}, u32[]{:S(2)}, u32[]{:S(2)}) collective-permute-start(bf16[4,80,128]{2,1,0:T(8,128)(2,1)} %get-tuple-element.18), channel_id=1, source_target_pairs={{0,16},{4,20},{8,24},{12,28},{16,32},{20,36},{24,40},{28,44},{32,4... | collective-permute-start | bytes 245768 | tf_op jit(solution)/shard_map/ppermute | solution.py:348
  64.5 6.6 %collective-permute-start.2 = (bf16[4,80,128]{2,1,0:T(8,128)(2,1)}, bf16[4,80,128]{2,1,0:T(8,128)(2,1)S(1)}, u32[]{:S(2)}, u32[]{:S(2)}) collective-permute-start(bf16[4,80,128]{2,1,0:T(8,128)(2,1)} %get-tuple-element.18), channel_id=1, source_target_pairs={{0,24},{4,28},{8,32},{12,36},{16,40},{20,44},{24,48},{28,52},{32,5... | collective-permute-start | bytes 245768 | tf_op jit(solution)/shard_map/ppermute | solution.py:348
  71.1 11.8 %collective-permute-start.23 = (bf16[13,80,128]{2,1,0:T(8,128)(2,1)}, bf16[13,80,128]{2,1,0:T(8,128)(2,1)S(1)}, u32[]{:S(2)}, u32[]{:S(2)}) collective-permute-start(bf16[13,80,128]{2,1,0:T(8,128)(2,1)} %get-tuple-element.19.own), channel_id=1, source_target_pairs={{0,3},{1,0},{2,1},{3,2},{4,7},{5,4},{6,5},{7,6},{8,11},{9,8},{10,9... | collective-permute-start | bytes 798728 | tf_op jit(solution)/shard_map/ppermute | solution.py:338
  73.8 10.3 %collective-permute-start.22 = (bf16[13,80,128]{2,1,0:T(8,128)(2,1)}, bf16[13,80,128]{2,1,0:T(8,128)(2,1)S(1)}, u32[]{:S(2)}, u32[]{:S(2)}) collective-permute-start(bf16[13,80,128]{2,1,0:T(8,128)(2,1)} %get-tuple-element.19.own), channel_id=1, source_target_pairs={{0,2},{1,3},{2,0},{3,1},{4,6},{5,7},{6,4},{7,5},{8,10},{9,11},{10,... | collective-permute-start | bytes 798728 | tf_op jit(solution)/shard_map/ppermute | solution.py:338
  74.4 23.6 %collective-permute-start.14 = (bf16[8,2,80,128]{3,2,1,0:T(8,128)(2,1)S(1)}, bf16[8,2,80,128]{3,2,1,0:T(8,128)(2,1)S(1)}, u32[]{:S(2)}, u32[]{:S(2)}) collective-permute-start(bf16[8,2,80,128]{3,2,1,0:T(8,128)(2,1)S(1)} %get-tuple-element.27.refs_1_), channel_id=1, source_target_pairs={{0,4},{4,0},{8,12},{12,8},{16,20},{20,16},{24,28},{28,24},{32,36},... | collective-permute-start | bytes 983048 | tf_op jit(solution)/shard_map/ppermute | solution.py:348
  80.8 17.7 %collective-permute-start.10 = (bf16[8,2,80,128]{3,2,1,0:T(8,128)(2,1)S(1)}, bf16[8,2,80,128]{3,2,1,0:T(8,128)(2,1)S(1)}, u32[]{:S(2)}, u32[]{:S(2)}) collective-permute-start(bf16[8,2,80,128]{3,2,1,0:T(8,128)(2,1)S(1)} %get-tuple-element.27.refs_1_), channel_id=1, source_target_pairs={{0,192},{4,196},{8,200},{12,204},{16,208},{20,212},{24,216},{28,22... | collective-permute-start | bytes 983048 | tf_op jit(solution)/shard_map/ppermute | solution.py:348
  82.8 16.1 %collective-permute-start.8 = (bf16[8,2,80,128]{3,2,1,0:T(8,128)(2,1)S(1)}, bf16[8,2,80,128]{3,2,1,0:T(8,128)(2,1)S(1)}, u32[]{:S(2)}, u32[]{:S(2)}) collective-permute-start(bf16[8,2,80,128]{3,2,1,0:T(8,128)(2,1)S(1)} %get-tuple-element.27.refs_1_), channel_id=1, source_target_pairs={{0,64},{4,68},{8,72},{12,76},{16,80},{20,84},{24,88},{28,92},{32,9... | collective-permute-start | bytes 983048 | tf_op jit(solution)/shard_map/ppermute | solution.py:348
  82.9 20.3 %collective-permute-start.7 = (bf16[8,2,80,128]{3,2,1,0:T(8,128)(2,1)S(1)}, bf16[8,2,80,128]{3,2,1,0:T(8,128)(2,1)S(1)}, u32[]{:S(2)}, u32[]{:S(2)}) collective-permute-start(bf16[8,2,80,128]{3,2,1,0:T(8,128)(2,1)S(1)} %get-tuple-element.28.refs_0_), channel_id=1, source_target_pairs={{0,64},{4,68},{8,72},{12,76},{16,80},{20,84},{24,88},{28,92},{32,9... | collective-permute-start | bytes 983048 | tf_op jit(solution)/shard_map/ppermute | solution.py:348
  84.1 7.6 %collective-permute-start.21 = (bf16[13,80,128]{2,1,0:T(8,128)(2,1)}, bf16[13,80,128]{2,1,0:T(8,128)(2,1)S(1)}, u32[]{:S(2)}, u32[]{:S(2)}) collective-permute-start(bf16[13,80,128]{2,1,0:T(8,128)(2,1)} %get-tuple-element.19.own), channel_id=1, source_target_pairs={{0,1},{1,2},{2,3},{3,0},{4,5},{5,6},{6,7},{7,4},{8,9},{9,10},{10,1... | collective-permute-start | bytes 798728 | tf_op jit(solution)/shard_map/ppermute | solution.py:338
  91.7 11.4 %collective-permute-start.13 = (bf16[8,2,80,128]{3,2,1,0:T(8,128)(2,1)S(1)}, bf16[8,2,80,128]{3,2,1,0:T(8,128)(2,1)S(1)}, u32[]{:S(2)}, u32[]{:S(2)}) collective-permute-start(bf16[8,2,80,128]{3,2,1,0:T(8,128)(2,1)S(1)} %get-tuple-element.28.refs_0_), channel_id=1, source_target_pairs={{0,4},{4,0},{8,12},{12,8},{16,20},{20,16},{24,28},{28,24},{32,36},... | collective-permute-start | bytes 983048 | tf_op jit(solution)/shard_map/ppermute | solution.py:348
  98.0 12.1 %collective-permute-start.12 = (bf16[8,2,80,128]{3,2,1,0:T(8,128)(2,1)S(1)}, bf16[8,2,80,128]{3,2,1,0:T(8,128)(2,1)S(1)}, u32[]{:S(2)}, u32[]{:S(2)}) collective-permute-start(bf16[8,2,80,128]{3,2,1,0:T(8,128)(2,1)S(1)} %get-tuple-element.28.refs_0_), channel_id=1, source_target_pairs={{0,192},{4,196},{8,200},{12,204},{16,208},{20,212},{24,216},{28,22... | collective-permute-start | bytes 983048 | tf_op jit(solution)/shard_map/ppermute | solution.py:348
  98.5 12.5 %collective-permute-start.20 = (bf16[8,2,80,128]{3,2,1,0:T(8,128)(2,1)S(1)}, bf16[8,2,80,128]{3,2,1,0:T(8,128)(2,1)S(1)}, u32[]{:S(2)}, u32[]{:S(2)}) collective-permute-start(bf16[8,2,80,128]{3,2,1,0:T(8,128)(2,1)S(1)} %collective-permute-done.10.refs_7_), channel_id=1, source_target_pairs={{0,4},{4,0},{8,12},{12,8},{16,20},{20,16},{24,28},{28,24},{32,36},... | collective-permute-start | bytes 983048 | tf_op jit(solution)/shard_map/ppermute | solution.py:348
  98.9 18.3 %collective-permute-start.11 = (bf16[8,2,80,128]{3,2,1,0:T(8,128)(2,1)S(1)}, bf16[8,2,80,128]{3,2,1,0:T(8,128)(2,1)S(1)}, u32[]{:S(2)}, u32[]{:S(2)}) collective-permute-start(bf16[8,2,80,128]{3,2,1,0:T(8,128)(2,1)S(1)} %collective-permute-done.10.refs_7_), channel_id=1, source_target_pairs={{0,192},{4,196},{8,200},{12,204},{16,208},{20,212},{24,216},{28,22... | collective-permute-start | bytes 983048 | tf_op jit(solution)/shard_map/ppermute | solution.py:348
  103.1 14.7 %collective-permute-start.9 = (bf16[8,2,80,128]{3,2,1,0:T(8,128)(2,1)S(1)}, bf16[8,2,80,128]{3,2,1,0:T(8,128)(2,1)S(1)}, u32[]{:S(2)}, u32[]{:S(2)}) collective-permute-start(bf16[8,2,80,128]{3,2,1,0:T(8,128)(2,1)S(1)} %collective-permute-done.7.refs_2_), channel_id=1, source_target_pairs={{0,64},{4,68},{8,72},{12,76},{16,80},{20,84},{24,88},{28,92},{32,9... | collective-permute-start | bytes 983048 | tf_op jit(solution)/shard_map/ppermute | solution.py:348
  103.2 18.9 %collective-permute-start.15 = (bf16[8,2,80,128]{3,2,1,0:T(8,128)(2,1)S(1)}, bf16[8,2,80,128]{3,2,1,0:T(8,128)(2,1)S(1)}, u32[]{:S(2)}, u32[]{:S(2)}) collective-permute-start(bf16[8,2,80,128]{3,2,1,0:T(8,128)(2,1)S(1)} %collective-permute-done.7.refs_2_), channel_id=1, source_target_pairs={{0,4},{4,0},{8,12},{12,8},{16,20},{20,16},{24,28},{28,24},{32,36},... | collective-permute-start | bytes 983048 | tf_op jit(solution)/shard_map/ppermute | solution.py:348
  110.1 11.9 %collective-permute-start.16 = (bf16[8,2,80,128]{3,2,1,0:T(8,128)(2,1)S(1)}, bf16[8,2,80,128]{3,2,1,0:T(8,128)(2,1)S(1)}, u32[]{:S(2)}, u32[]{:S(2)}) collective-permute-start(bf16[8,2,80,128]{3,2,1,0:T(8,128)(2,1)S(1)} %collective-permute-done.8.refs_3_), channel_id=1, source_target_pairs={{0,4},{4,0},{8,12},{12,8},{16,20},{20,16},{24,28},{28,24},{32,36},... | collective-permute-start | bytes 983048 | tf_op jit(solution)/shard_map/ppermute | solution.py:348
  111.1 11.0 %collective-permute-start.19 = (bf16[8,2,80,128]{3,2,1,0:T(8,128)(2,1)S(1)}, bf16[8,2,80,128]{3,2,1,0:T(8,128)(2,1)S(1)}, u32[]{:S(2)}, u32[]{:S(2)}) collective-permute-start(bf16[8,2,80,128]{3,2,1,0:T(8,128)(2,1)S(1)} %collective-permute-done.12.refs_6_), channel_id=1, source_target_pairs={{0,4},{4,0},{8,12},{12,8},{16,20},{20,16},{24,28},{28,24},{32,36},... | collective-permute-start | bytes 983048 | tf_op jit(solution)/shard_map/ppermute | solution.py:348
  117.2 5.0 %collective-permute-start.18 = (bf16[8,2,80,128]{3,2,1,0:T(8,128)(2,1)S(1)}, bf16[8,2,80,128]{3,2,1,0:T(8,128)(2,1)S(1)}, u32[]{:S(2)}, u32[]{:S(2)}) collective-permute-start(bf16[8,2,80,128]{3,2,1,0:T(8,128)(2,1)S(1)} %collective-permute-done.11.refs_5_), channel_id=1, source_target_pairs={{0,4},{4,0},{8,12},{12,8},{16,20},{20,16},{24,28},{28,24},{32,36},... | collective-permute-start | bytes 983048 | tf_op jit(solution)/shard_map/ppermute | solution.py:348
  149.6 9.3 %collective-permute-start.24 = (bf16[13,80,128]{2,1,0:T(8,128)(2,1)}, bf16[13,80,128]{2,1,0:T(8,128)(2,1)S(1)}, u32[]{:S(2)}, u32[]{:S(2)}) collective-permute-start(bf16[13,80,128]{2,1,0:T(8,128)(2,1)} %get-tuple-element.21), channel_id=1, source_target_pairs={{0,1},{1,2},{2,3},{3,0},{4,5},{5,6},{6,7},{7,4},{8,9},{9,10},{10,1... | collective-permute-start | bytes 798728 | tf_op jit(solution)/shard_map/ppermute | solution.py:338
  149.7 15.2 %collective-permute-start.25 = (bf16[13,80,128]{2,1,0:T(8,128)(2,1)}, bf16[13,80,128]{2,1,0:T(8,128)(2,1)S(1)}, u32[]{:S(2)}, u32[]{:S(2)}) collective-permute-start(bf16[13,80,128]{2,1,0:T(8,128)(2,1)} %get-tuple-element.22), channel_id=1, source_target_pairs={{0,2},{1,3},{2,0},{3,1},{4,6},{5,7},{6,4},{7,5},{8,10},{9,11},{10,... | collective-permute-start | bytes 798728 | tf_op jit(solution)/shard_map/ppermute | solution.py:338
  152.7 12.3 %collective-permute-start.26 = (bf16[13,80,128]{2,1,0:T(8,128)(2,1)}, bf16[13,80,128]{2,1,0:T(8,128)(2,1)S(1)}, u32[]{:S(2)}, u32[]{:S(2)}) collective-permute-start(bf16[13,80,128]{2,1,0:T(8,128)(2,1)} %get-tuple-element.23), channel_id=1, source_target_pairs={{0,3},{1,0},{2,1},{3,2},{4,7},{5,4},{6,5},{7,6},{8,11},{9,8},{10,9... | collective-permute-start | bytes 798728 | tf_op jit(solution)/shard_map/ppermute | solution.py:338
  201.9 10.3 %collective-permute-start.27 = (bf16[3,32,1664]{2,1,0:T(8,128)(2,1)}, bf16[3,32,1664]{2,1,0:T(8,128)(2,1)S(1)}, u32[]{:S(2)}, u32[]{:S(2)}) collective-permute-start(bf16[3,32,1664]{2,1,0:T(8,128)(2,1)} %get-tuple-element.25.refs_0_), channel_id=1, source_target_pairs={{0,1},{1,2},{2,3},{3,0},{4,5},{5,6},{6,7},{7,4},{8,9},{9,10},{10,1... | collective-permute-start | bytes 958472 | tf_op jit(solution)/shard_map/ppermute | solution.py:338
  201.9 10.3 %collective-permute-start.30 = (bf16[3,32,1664]{2,1,0:T(8,128)(2,1)}, bf16[3,32,1664]{2,1,0:T(8,128)(2,1)S(1)}, u32[]{:S(2)}, u32[]{:S(2)}) collective-permute-start(bf16[3,32,1664]{2,1,0:T(8,128)(2,1)} %get-tuple-element.26.refs_1_), channel_id=1, source_target_pairs={{0,3},{1,0},{2,1},{3,2},{4,7},{5,4},{6,5},{7,6},{8,11},{9,8},{10,9... | collective-permute-start | bytes 958472 | tf_op jit(solution)/shard_map/ppermute | solution.py:338
  204.5 13.5 %collective-permute-start.32 = (bf16[3,32,1664]{2,1,0:T(8,128)(2,1)}, bf16[3,32,1664]{2,1,0:T(8,128)(2,1)S(1)}, u32[]{:S(2)}, u32[]{:S(2)}) collective-permute-start(bf16[3,32,1664]{2,1,0:T(8,128)(2,1)} %get-tuple-element.25.refs_0_), channel_id=1, source_target_pairs={{0,3},{1,0},{2,1},{3,2},{4,7},{5,4},{6,5},{7,6},{8,11},{9,8},{10,9... | collective-permute-start | bytes 958472 | tf_op jit(solution)/shard_map/ppermute | solution.py:338
  205.4 13.5 %collective-permute-start.28 = (bf16[3,32,1664]{2,1,0:T(8,128)(2,1)}, bf16[3,32,1664]{2,1,0:T(8,128)(2,1)S(1)}, u32[]{:S(2)}, u32[]{:S(2)}) collective-permute-start(bf16[3,32,1664]{2,1,0:T(8,128)(2,1)} %get-tuple-element.26.refs_1_), channel_id=1, source_target_pairs={{0,1},{1,2},{2,3},{3,0},{4,5},{5,6},{6,7},{7,4},{8,9},{9,10},{10,1... | collective-permute-start | bytes 958472 | tf_op jit(solution)/shard_map/ppermute | solution.py:338
  212.1 13.7 %collective-permute-start.29 = (bf16[3,32,1664]{2,1,0:T(8,128)(2,1)S(1)}, bf16[3,32,1664]{2,1,0:T(8,128)(2,1)S(1)}, u32[]{:S(2)}, u32[]{:S(2)}) collective-permute-start(bf16[3,32,1664]{2,1,0:T(8,128)(2,1)S(1)} %collective-permute-done.27.refs_2_), channel_id=1, source_target_pairs={{0,1},{1,2},{2,3},{3,0},{4,5},{5,6},{6,7},{7,4},{8,9},{9,10},{10,1... | collective-permute-start | bytes 958472 | tf_op jit(solution)/shard_map/ppermute | solution.py:338
  212.1 13.7 %collective-permute-start.31 = (bf16[3,32,1664]{2,1,0:T(8,128)(2,1)S(1)}, bf16[3,32,1664]{2,1,0:T(8,128)(2,1)S(1)}, u32[]{:S(2)}, u32[]{:S(2)}) collective-permute-start(bf16[3,32,1664]{2,1,0:T(8,128)(2,1)S(1)} %collective-permute-done.30.refs_7_), channel_id=1, source_target_pairs={{0,3},{1,0},{2,1},{3,2},{4,7},{5,4},{6,5},{7,6},{8,11},{9,8},{10,9... | collective-permute-start | bytes 958472 | tf_op jit(solution)/shard_map/ppermute | solution.py:338
  (29 other events, 392.9 us)

commit v3 on v2

--- a/solution.py
+++ b/solution.py
@@ -19,6 +19,10 @@
 GROUPS = 4
 ROWS_T = 40
 ROWS_S = 16
+EACH = 3
+WHOLE = EACH * BANDS
+REST = 10
+PIECE = 256
 ROWS_M = ROWS_T + ROWS_S
 HALF = BANDS // 2
 PITCH = 88
@@ -117,8 +121,16 @@
         for u in range(TILES // 2):
             got = dot(pick, stick[c, :, u * 256 : u * 256 + 256])
             for h in range(2):
-                row = (2 * u + h) * ROWS_S + c * SRC
-                scr_s[row : row + SRC, :] = got[:SRC, h * LANES : (h + 1) * LANES]
+                for k in range(SRC):
+                    flat = k * TILES + 2 * u + h
+                    line = got[k : k + 1, h * LANES : (h + 1) * LANES]
+                    if flat < WHOLE:
+                        places = [(flat // EACH, flat % EACH)]
+                    else:
+                        places = [(8 * (flat - WHOLE) + i, EACH) for i in range(8)]
+                    for d, r in places:
+                        row = d * ROWS_S + c * SRC + r
+                        scr_s[row : row + 1, :] = line
 
     def out_body(b, _):
         mine = scr[pl.ds(b, ROWS_T, stride=BANDS), :]
@@ -129,20 +141,29 @@
     lax.fori_loop(0, BANDS, out_body, 0, unroll=8)
 
 
-def rows_kernel(got, sel, quarter, piece, scr):
+def rows_kernel(got, sel, quarter, piece, scr, last):
     def load(d, _):
         scr[pl.ds(pl.multiple_of(d * ROWS_M, 8), ROWS_M), :] = got[d].astype(F32)
         return 0
 
     lax.fori_loop(0, BANDS, load, 0, unroll=8)
     tables = [sel[c] for c in range(SLOTS)]
-    for out, count, first in ((piece, SRC, ROWS_T), (quarter, QUART, 0)):
-        for t in range(count):
-            total = jnp.zeros((N, LANES), F32)
-            for c in range(SLOTS):
-                rows = scr[pl.ds(first + c * count + t, BANDS, stride=ROWS_M), :].astype(BF)
-                total = total + dot(tables[c], rows)
-            out[t] = total.astype(BF)
+
+    def contracted(first, count, t):
+        total = jnp.zeros((N, LANES), F32)
+        for c in range(SLOTS):
+            rows = scr[pl.ds(first + c * count + t, BANDS, stride=ROWS_M), :].astype(BF)
+            total = total + dot(tables[c], rows)
+        return total
+
+    for r in range(EACH):
+        piece[r * N : (r + 1) * N, :] = contracted(ROWS_T, SRC, r).astype(BF)
+    last[:N, :] = contracted(ROWS_T, SRC, EACH)
+    last[N:, :] = jnp.zeros((16, LANES), F32)
+    band = lax.axis_index("band")
+    piece[EACH * N :, :] = last[pl.ds((band & 7) * REST, 16), :].astype(BF)
+    for t in range(QUART):
+        quarter[t] = contracted(0, QUART, t).astype(BF)
 
 
 def turned(scr, index):
@@ -193,19 +214,24 @@
     to_real(lambda t: quarters[t], out, table, expand, scr)
 
 
-def gather_tiles(same_core, other_core, pieces):
+def gather_tiles(groups, pieces, rest):
     band = lax.axis_index("band")
     core, z_at, x_at = band & 1, (band >> 1) & 7, band >> 4
-    for kx in range(4):
-        for kz in range(8):
-            origin = (((x_at - kx) & 3) * 8 + ((z_at - kz) & 7)) * 2
-            for e in range(2):
-                pieces[origin + core, 2 * e : 2 * e + 2] = same_core[2 * kx + e][kz]
-                pieces[origin + 1 - core, 2 * e : 2 * e + 2] = other_core[2 * kx + e][kz]
+    for ref, kx, flip, places in groups:
+        for j, (back, swap) in enumerate(places):
+            z = (z_at - back) & 7
+            z = (z ^ 1) if swap else z
+            origin = (((x_at - kx) & 3) * 8 + z) * 2 + (core ^ flip)
+            whole = ref[j // 2, j % 2]
+            for r in range(EACH):
+                pieces[origin * EACH + r] = whole[r * N : (r + 1) * N]
+            rest[pl.ds(origin * REST, REST), :] = whole[EACH * N :].astype(F32)[:REST]
+    for j in range(SRC * TILES - WHOLE):
+        pieces[WHOLE + j] = rest[j * N : (j + 1) * N, :].astype(BF)
 
 
 def one_source(pieces, k, target, source, partial, table, expand, twin, screen, scr_a, scr_b):
-    to_real(lambda t: pieces[t, k], source, table, expand, scr_a)
+    to_real(lambda t: pieces[k * TILES + t], source, table, expand, scr_a)
     h = table[...]
     turn = twin[...]
     for lead in range(0, N, 2 * CHUNK):
@@ -253,12 +279,17 @@
 
 
 def pairs_kernel(*refs):
-    same_core, other_core = refs[:8], refs[8:16]
-    target, table, expand, twin, c0, c1, c2, screen = refs[16:24]
-    outs = refs[24:28]
-    source, partial, scr_a, scr_b, final, pieces = refs[28:]
+    target, table, expand, twin, c0, c1, c2, screen = refs[10:18]
+    outs = refs[18:22]
+    source, partial, scr_a, scr_b, final, pieces, rest = refs[22:]
     g = lax.axis_index("grp")
-    gather_tiles(same_core, other_core, pieces)
+    places = [(back, swap) for back in (0, 2, 4, 6) for swap in (False, True)]
+    groups = []
+    for flip in range(2):
+        own, ahead, behind, far_a, far_b = refs[5 * flip : 5 * flip + 5]
+        groups += [(own, 0, flip, places), (ahead, 1, flip, places), (behind, 3, flip, places)]
+        groups += [(far_a, 2, flip, places[:4]), (far_b, 2, flip, places[4:])]
+    gather_tiles(groups, pieces, rest)
     partial[...] = jnp.zeros_like(partial)
 
     def body(k, _):
@@ -336,6 +367,11 @@
 
 def shift_grp(value, k):
     return lax.ppermute(value, "grp", [(i, (i + k) % GROUPS) for i in range(GROUPS)])
+
+
+def swap_band(value, axis):
+    bit = {"core": 1, "z": 2}[axis]
+    return lax.ppermute(value, "band", [(i, i ^ bit) for i in range(BANDS)])
 
 
 def shift_band(value, dx, dz, dc):
@@ -380,19 +416,20 @@
     got = lax.all_to_all(msg, "band", 0, 0, tiled=True)
     quarter, piece = pl.pallas_call(
         rows_kernel,
-        out_shape=(shape((QUART, N, LANES)), shape((SRC, N, LANES))),
+        out_shape=(shape((QUART, N, LANES)), shape((PIECE, LANES))),
         in_specs=[VM, VM],
         out_specs=(VM, VM),
-        scratch_shapes=[pltpu.VMEM((ROWS_M * BANDS, LANES), F32)],
+        scratch_shapes=[
+            pltpu.VMEM((ROWS_M * BANDS, LANES), F32),
+            pltpu.VMEM((N + 16, LANES), F32),
+        ],
         compiler_params=PARAMS,
     )(got, sel)
 
-    along_z = [piece] + [shift_band(piece, 0, k, 0) for k in range(1, 8)]
+    swapped = swap_band(piece, "z")
     quarters = [quarter] + [shift_grp(quarter, k) for k in range(1, 4)]
-    halves = [jnp.stack([v[2 * e : 2 * e + 2] for v in along_z]) for e in range(2)]
-    gathered = ring_gather(*halves, lambda v, k: shift_band(v, k, 0, 0))
-    same_core = [v for both in gathered for v in both]
-    other_core = [shift_band(v, 0, 0, 1) for v in same_core]
+    couple = jnp.stack([piece, swapped])
+    along_z = jnp.stack([couple] + [shift_band(couple, 0, k, 0) for k in (2, 4, 6)])
 
     target = pl.pallas_call(
         target_kernel,
@@ -406,10 +443,16 @@
         compiler_params=PARAMS,
     )(*quarters, table, expand)
 
+    along_z, target = lax.optimization_barrier((along_z, target))
+    ahead, behind = shift_band(along_z, 1, 0, 0), shift_band(along_z, 3, 0, 0)
+    far_a, far_b = shift_band(ahead[:2], 1, 0, 0), shift_band(behind[2:], 3, 0, 0)
+    same_core = [along_z, ahead, behind, far_a, far_b]
+    other_core = [shift_band(v, 0, 0, 1) for v in same_core]
+
     outs = pl.pallas_call(
         pairs_kernel,
         out_shape=tuple(shape((QUART, N, LANES)) for _ in range(4)),
-        in_specs=[VM] * 24,
+        in_specs=[VM] * 18,
         out_specs=(VM,) * 4,
         scratch_shapes=[
             pltpu.VMEM((N, N, LANES), BF),
@@ -417,7 +460,8 @@
             pltpu.VMEM((N * PITCH, LANES), F32),
             pltpu.VMEM((N * PITCH, LANES), F32),
             pltpu.VMEM((TILES + 2, N, LANES), BF),
-            pltpu.VMEM((BANDS, SRC, N, LANES), BF),
+            pltpu.VMEM((SRC * TILES, N, LANES), BF),
+            pltpu.VMEM((BANDS * REST, LANES), F32),
         ],
         compiler_params=PARAMS,
     )(*same_core, *other_core, target, table, expand, twin, c0, c1, c2, screen)

time: 231 us -> 208 us (0.900)
  starting transfers between devices: 45.1 us -> 34.4 us
  waiting for transfers between devices: 65.5 us -> 56.8 us
  blocking collectives: 69.5 us -> 65.6 us
    ppermute x21 -> x12, starting transfers between devices: 31.4 us -> 19.2 us  [shift_band(): return lax.ppermute(value, 'band', moves)]
    ppermute x21 -> x12, waiting for transfers between devices: 29.2 us -> 19.2 us  [shift_band(): return lax.ppermute(value, 'band', moves)]
    all_to_all x1, blocking collectives: 30.6 us -> 26.8 us  [shards(): received = lax.all_to_all(message, 'band', 0, 0, tiled=True)]
    ppermute x0 -> x1, waiting for transfers between devices: none -> 2.75 us  [swap_band(): return lax.ppermute(value, 'band', [(i, i ^ bit) for i in range(BANDS)])]
    unnamed x63 -> x44, local copies, waits for them, and re-layouts: 4.84 us -> 4.59 us
  transfers between devices with their start and end apart: 33 -> 25, of which waited for: 12 -> 15; matrix products, arithmetic and copies ran while one was open for 0% -> 0% of each run, Pallas kernels for 2% -> 0%
where the time goes in v3:
time: 208 us
  blocking collectives  65.6 us (32%)
  waiting for transfers between devices  56.8 us (27%)
  Pallas kernels  44.9 us (22%)
  starting transfers between devices  34.4 us (17%)
  local copies, waits for them, and re-layouts  4.62 us (2%)
    all_to_all x1, blocking collectives, shards(): got = lax.all_to_all(msg, 'band', 0, 0, tiled=True)  38.8 us
    ppermute x12, waiting for transfers between devices, shift_grp(): lax.ppermute(value, 'grp', [(i, (i + k) % GROUPS) for i in range(GROUPS)])  34.8 us
    all_to_all x1, blocking collectives, shards(): received = lax.all_to_all(message, 'band', 0, 0, tiled=True)  26.8 us
    pallas_call x1, Pallas kernels, shards(): pl.pallas_call(pairs_kernel, out_shape=tuple((shape((QUART, N, LANES)) fo...  25.4 us
    ppermute x12, waiting for transfers between devices, shift_band(): return lax.ppermute(value, 'band', moves)  19.2 us
    ppermute x12, starting transfers between devices, shift_band(): return lax.ppermute(value, 'band', moves)  19.2 us
    ppermute x12, starting transfers between devices, shift_grp(): lax.ppermute(value, 'grp', [(i, (i + k) % GROUPS) for i in range(GROUPS)])  14.7 us
    unnamed x44, local copies, waits for them, and re-layouts  4.59 us
  transfers between devices with their start and end apart: 25, of which 15 were waited for; matrix products, arithmetic and copies ran while one was open for 0% of the time, Pallas kernels for 0%

profile of v3, /device:TPU:1, one launch (start us, length us, event | category | flops | bytes accessed | tf_op | source)
XLA Modules:
  0.0 207.6 jit_solution(7009423784754912790)
XLA Ops:
  0.0 4.2 %shard_map.109 = (bf16[64,56,128]{2,1,0:T(8,128)(2,1)}, bf16[3,80,64]{2,1,0:T(8,128)(2,1)}, bf16[3,64,80]{2,1,0:T(8,128)(2,1)}) custom-call(s32[64]{0:T(128)} %order_s.1, bf16[3,64,6400]{2,1,0:T(8,128)(2,1)} %stick.1, s32[1,64]{1,0:T(1,128)} %bitcast.14, s32[1,80]{1,0:T(1,128)} %bitcast.15, bf16[80,80]{1,0:T(8,128)(2,1)} %constant.14.clone.table.refs_11_), custom_call_target="tpu_custom_call" | custom-call | tf_op jit(solution)/shard_map/pallas_call | solution.py:401
  4.2 38.8 %all_to_all.10.got = bf16[64,56,128]{2,1,0:T(8,128)(2,1)} all-to-all(bf16[64,56,128]{2,1,0:T(8,128)(2,1)} %get-tuple-element.18), channel_id=1, replica_groups=mesh['band'=64,'grp'=4] {'band'}, dimensions={0} | all-to-all | bytes 1835008 | tf_op jit(solution)/shard_map/all_to_all | solution.py:416
  43.0 2.7 %shard_map.110 = (bf16[13,80,128]{2,1,0:T(8,128)(2,1)}, bf16[256,128]{1,0:T(8,128)(2,1)}) custom-call(bf16[64,56,128]{2,1,0:T(8,128)(2,1)} %all_to_all.10.got, bf16[3,80,64]{2,1,0:T(8,128)(2,1)} %get-tuple-element.19.sel), custom_call_target="tpu_custom_call" | custom-call | tf_op jit(solution)/shard_map/pallas_call | solution.py:417
  46.3 2.7 %collective-permute-done = bf16[256,128]{1,0:T(8,128)(2,1)S(1)} collective-permute-done((bf16[256,128]{1,0:T(8,128)(2,1)}, bf16[256,128]{1,0:T(8,128)(2,1)S(1)}, u32[]{:S(2)}, u32[]{:S(2)}) %collective-permute-start) | collective-permute-done | bytes 65568 | tf_op jit(solution)/shard_map/ppermute | solution.py:374
  49.9 2.8 %collective-permute-start.2 = (bf16[2,256,128]{2,1,0:T(8,128)(2,1)S(1)}, bf16[2,256,128]{2,1,0:T(8,128)(2,1)S(1)}, u32[]{:S(2)}, u32[]{:S(2)}) collective-permute-start(bf16[2,256,128]{2,1,0:T(8,128)(2,1)S(1)} %get-tuple-element.32), channel_id=1, source_target_pairs={{0,32},{4,36},{8,40},{12,44},{16,48},{20,52},{24,56},{28,60},{32,0... | collective-permute-start | bytes 393224 | tf_op jit(solution)/shard_map/ppermute | solution.py:384
  52.7 2.7 %collective-permute-start.6 = (bf16[13,80,128]{2,1,0:T(8,128)(2,1)}, bf16[13,80,128]{2,1,0:T(8,128)(2,1)S(1)}, u32[]{:S(2)}, u32[]{:S(2)}) collective-permute-start(bf16[13,80,128]{2,1,0:T(8,128)(2,1)} %get-tuple-element.21.own), channel_id=1, source_target_pairs={{0,3},{1,0},{2,1},{3,2},{4,7},{5,4},{6,5},{7,6},{8,11},{9,8},{10,9... | collective-permute-start | bytes 798728 | tf_op jit(solution)/shard_map/ppermute | solution.py:369
  57.0 2.7 %collective-permute-done.2 = bf16[2,256,128]{2,1,0:T(8,128)(2,1)S(1)} collective-permute-done((bf16[2,256,128]{2,1,0:T(8,128)(2,1)S(1)}, bf16[2,256,128]{2,1,0:T(8,128)(2,1)S(1)}, u32[]{:S(2)}, u32[]{:S(2)}) %collective-permute-start.2) | collective-permute-done | bytes 131104 | tf_op jit(solution)/shard_map/ppermute | solution.py:384
  60.1 2.9 %collective-permute-done.1 = bf16[2,256,128]{2,1,0:T(8,128)(2,1)S(1)} collective-permute-done((bf16[2,256,128]{2,1,0:T(8,128)(2,1)S(1)}, bf16[2,256,128]{2,1,0:T(8,128)(2,1)S(1)}, u32[]{:S(2)}, u32[]{:S(2)}) %collective-permute-start.1) | collective-permute-done | bytes 131104 | tf_op jit(solution)/shard_map/ppermute | solution.py:384
  63.0 1.8 collective-permute-done.3
  64.9 6.3 %collective-permute-done.4.got1 = bf16[13,80,128]{2,1,0:T(8,128)(2,1)S(1)} collective-permute-done((bf16[13,80,128]{2,1,0:T(8,128)(2,1)}, bf16[13,80,128]{2,1,0:T(8,128)(2,1)S(1)}, u32[]{:S(2)}, u32[]{:S(2)}) %collective-permute-start.4) | collective-permute-done | bytes 266272 | tf_op jit(solution)/shard_map/ppermute | solution.py:369
  71.9 3.9 %shard_map.111.refs_10_ = bf16[80,80,128]{2,1,0:T(8,128)(2,1)} custom-call(bf16[13,80,128]{2,1,0:T(8,128)(2,1)} %get-tuple-element.21.own, bf16[13,80,128]{2,1,0:T(8,128)(2,1)} %copy-done.14, bf16[13,80,128]{2,1,0:T(8,128)(2,1)} %copy-done.13, bf16[13,80,128]{2,1,0:T(8,128)(2,1)} %copy-done.12, bf16[80,80]{1,0:T(8,128)(2,1)} %constant.14.clone.table.refs_11_, ...), custom_call_target="tpu_custom_call" | custom-call | tf_op jit(solution)/shard_map/pallas_call | solution.py:434
  75.8 2.4 %collective-permute-start.8 = (bf16[4,2,256,128]{3,2,1,0:T(8,128)(2,1)S(1)}, bf16[4,2,256,128]{3,2,1,0:T(8,128)(2,1)S(1)}, u32[]{:S(2)}, u32[]{:S(2)}) collective-permute-start(bf16[4,2,256,128]{3,2,1,0:T(8,128)(2,1)S(1)} %pad_maximum_fusion.refs_0_), channel_id=1, source_target_pairs={{0,192},{4,196},{8,200},{12,204},{16,208},{20,212},{24,216},{28,22... | collective-permute-start | bytes 1572872 | tf_op jit(solution)/shard_map/ppermute | solution.py:384
  78.3 1.3 collective-permute-start.11
  79.6 9.3 %collective-permute-done.8.refs_2_ = bf16[4,2,256,128]{3,2,1,0:T(8,128)(2,1)S(1)} collective-permute-done((bf16[4,2,256,128]{3,2,1,0:T(8,128)(2,1)S(1)}, bf16[4,2,256,128]{3,2,1,0:T(8,128)(2,1)S(1)}, u32[]{:S(2)}, u32[]{:S(2)}) %collective-permute-start.8) | collective-permute-done | bytes 524320 | tf_op jit(solution)/shard_map/ppermute | solution.py:384
  88.9 3.2 %collective-permute-start.10 = (bf16[2,2,256,128]{3,2,1,0:T(8,128)(2,1)S(1)}, bf16[2,2,256,128]{3,2,1,0:T(8,128)(2,1)S(1)}, u32[]{:S(2)}, u32[]{:S(2)}) collective-permute-start(bf16[2,2,256,128]{3,2,1,0:T(8,128)(2,1)S(1)} %slice.9), channel_id=1, source_target_pairs={{0,192},{4,196},{8,200},{12,204},{16,208},{20,212},{24,216},{28,22... | collective-permute-start | bytes 786440 | tf_op jit(solution)/shard_map/ppermute | solution.py:384
  92.1 2.5 %collective-permute-start.13 = (bf16[4,2,256,128]{3,2,1,0:T(8,128)(2,1)S(1)}, bf16[4,2,256,128]{3,2,1,0:T(8,128)(2,1)S(1)}, u32[]{:S(2)}, u32[]{:S(2)}) collective-permute-start(bf16[4,2,256,128]{3,2,1,0:T(8,128)(2,1)S(1)} %collective-permute-done.8.refs_2_), channel_id=1, source_target_pairs={{0,4},{4,0},{8,12},{12,8},{16,20},{20,16},{24,28},{28,24},{32,36},... | collective-permute-start | bytes 1572872 | tf_op jit(solution)/shard_map/ppermute | solution.py:384
  95.7 2.8 %collective-permute-start.15 = (bf16[2,2,256,128]{3,2,1,0:T(8,128)(2,1)S(1)}, bf16[2,2,256,128]{3,2,1,0:T(8,128)(2,1)S(1)}, u32[]{:S(2)}, u32[]{:S(2)}) collective-permute-start(bf16[2,2,256,128]{3,2,1,0:T(8,128)(2,1)S(1)} %collective-permute-done.10.refs_4_), channel_id=1, source_target_pairs={{0,4},{4,0},{8,12},{12,8},{16,20},{20,16},{24,28},{28,24},{32,36},... | collective-permute-start | bytes 786440 | tf_op jit(solution)/shard_map/ppermute | solution.py:384
  98.9 3.1 %collective-permute-start.14 = (bf16[2,2,256,128]{3,2,1,0:T(8,128)(2,1)S(1)}, bf16[2,2,256,128]{3,2,1,0:T(8,128)(2,1)S(1)}, u32[]{:S(2)}, u32[]{:S(2)}) collective-permute-start(bf16[2,2,256,128]{3,2,1,0:T(8,128)(2,1)S(1)} %collective-permute-done.9.refs_3_), channel_id=1, source_target_pairs={{0,4},{4,0},{8,12},{12,8},{16,20},{20,16},{24,28},{28,24},{32,36},... | collective-permute-start | bytes 786440 | tf_op jit(solution)/shard_map/ppermute | solution.py:384
  102.1 1.1 collective-permute-done.14.refs_8_
  104.9 25.4 %shard_map.112 = (bf16[13,80,128]{2,1,0:T(8,128)(2,1)}, bf16[13,80,128]{2,1,0:T(8,128)(2,1)}, bf16[13,80,128]{2,1,0:T(8,128)(2,1)}, bf16[13,80,128]{2,1,0:T(8,128)(2,1)}) custom-call(bf16[4,2,256,128]{3,2,1,0:T(8,128)(2,1)} %copy-done, bf16[4,2,256,128]{3,2,1,0:T(8,128)(2,1)} %copy-done.2, bf16[4,2,256,128]{3,2,1,0:T(8,128)(2,1)} %copy-done.1, ...), custom_call_target="tpu_custom_call" | custom-call | tf_op jit(solution)/shard_map/pallas_call | solution.py:452
  131.0 2.8 %collective-permute-start.17 = (bf16[13,80,128]{2,1,0:T(8,128)(2,1)}, bf16[13,80,128]{2,1,0:T(8,128)(2,1)S(1)}, u32[]{:S(2)}, u32[]{:S(2)}) collective-permute-start(bf16[13,80,128]{2,1,0:T(8,128)(2,1)} %get-tuple-element.26), channel_id=1, source_target_pairs={{0,2},{1,3},{2,0},{3,1},{4,6},{5,7},{6,4},{7,5},{8,10},{9,11},{10,... | collective-permute-start | bytes 798728 | tf_op jit(solution)/shard_map/ppermute | solution.py:369
  134.4 4.9 %collective-permute-done.16.got1 = bf16[13,80,128]{2,1,0:T(8,128)(2,1)S(1)} collective-permute-done((bf16[13,80,128]{2,1,0:T(8,128)(2,1)}, bf16[13,80,128]{2,1,0:T(8,128)(2,1)S(1)}, u32[]{:S(2)}, u32[]{:S(2)}) %collective-permute-start.16) | collective-permute-done | bytes 266272 | tf_op jit(solution)/shard_map/ppermute | solution.py:369
  139.3 6.5 %collective-permute-done.17.got2 = bf16[13,80,128]{2,1,0:T(8,128)(2,1)S(1)} collective-permute-done((bf16[13,80,128]{2,1,0:T(8,128)(2,1)}, bf16[13,80,128]{2,1,0:T(8,128)(2,1)S(1)}, u32[]{:S(2)}, u32[]{:S(2)}) %collective-permute-start.17) | collective-permute-done | bytes 266272 | tf_op jit(solution)/shard_map/ppermute | solution.py:369
  146.6 3.2 %shard_map.113 = bf16[64,40,128]{2,1,0:T(8,128)(2,1)} custom-call(bf16[13,80,128]{2,1,0:T(8,128)(2,1)} %get-tuple-element.24.own, bf16[13,80,128]{2,1,0:T(8,128)(2,1)} %copy-done.15, bf16[13,80,128]{2,1,0:T(8,128)(2,1)} %copy-done.16, bf16[13,80,128]{2,1,0:T(8,128)(2,1)} %copy-done.17, bf16[3,64,80]{2,1,0:T(8,128)(2,1)} %get-tuple-element.28.sel_t), custom_call_target="tpu_custom_call" | custom-call | tf_op jit(solution)/shard_map/pallas_call | solution.py:470
  149.8 26.8 %all_to_all.11.got = bf16[64,40,128]{2,1,0:T(8,128)(2,1)} all-to-all(bf16[64,40,128]{2,1,0:T(8,128)(2,1)} %shard_map.113), channel_id=1, replica_groups=mesh['band'=64,'grp'=4] {'band'}, dimensions={0} | all-to-all | bytes 1310720 | tf_op jit(solution)/shard_map/all_to_all | solution.py:479
  176.6 2.3 %shard_map.114 = (bf16[3,32,1664]{2,1,0:T(8,128)(2,1)}, bf16[3,32,1664]{2,1,0:T(8,128)(2,1)}) custom-call(bf16[64,40,128]{2,1,0:T(8,128)(2,1)} %all_to_all.11.got), custom_call_target="tpu_custom_call" | custom-call | tf_op jit(solution)/shard_map/pallas_call | solution.py:480
  179.4 2.2 %collective-permute-start.22 = (bf16[3,32,1664]{2,1,0:T(8,128)(2,1)}, bf16[3,32,1664]{2,1,0:T(8,128)(2,1)S(1)}, u32[]{:S(2)}, u32[]{:S(2)}) collective-permute-start(bf16[3,32,1664]{2,1,0:T(8,128)(2,1)} %get-tuple-element.30.refs_1_), channel_id=1, source_target_pairs={{0,3},{1,0},{2,1},{3,2},{4,7},{5,4},{6,5},{7,6},{8,11},{9,8},{10,9... | collective-permute-start | bytes 958472 | tf_op jit(solution)/shard_map/ppermute | solution.py:369
  183.1 6.1 %collective-permute-done.19.refs_2_ = bf16[3,32,1664]{2,1,0:T(8,128)(2,1)S(1)} collective-permute-done((bf16[3,32,1664]{2,1,0:T(8,128)(2,1)}, bf16[3,32,1664]{2,1,0:T(8,128)(2,1)S(1)}, u32[]{:S(2)}, u32[]{:S(2)}) %collective-permute-start.19) | collective-permute-done | bytes 319520 | tf_op jit(solution)/shard_map/ppermute | solution.py:369
  189.2 2.7 %collective-permute-start.23 = (bf16[3,32,1664]{2,1,0:T(8,128)(2,1)S(1)}, bf16[3,32,1664]{2,1,0:T(8,128)(2,1)S(1)}, u32[]{:S(2)}, u32[]{:S(2)}) collective-permute-start(bf16[3,32,1664]{2,1,0:T(8,128)(2,1)S(1)} %collective-permute-done.22.refs_7_), channel_id=1, source_target_pairs={{0,3},{1,0},{2,1},{3,2},{4,7},{5,4},{6,5},{7,6},{8,11},{9,8},{10,9... | collective-permute-start | bytes 958472 | tf_op jit(solution)/shard_map/ppermute | solution.py:369
  191.9 3.2 %collective-permute-done.24.refs_6_ = bf16[3,32,1664]{2,1,0:T(8,128)(2,1)S(1)} collective-permute-done((bf16[3,32,1664]{2,1,0:T(8,128)(2,1)}, bf16[3,32,1664]{2,1,0:T(8,128)(2,1)S(1)}, u32[]{:S(2)}, u32[]{:S(2)}) %collective-permute-start.24) | collective-permute-done | bytes 319520 | tf_op jit(solution)/shard_map/ppermute | solution.py:369
  196.0 6.8 %collective-permute-done.21.refs_4_ = bf16[3,32,1664]{2,1,0:T(8,128)(2,1)S(1)} collective-permute-done((bf16[3,32,1664]{2,1,0:T(8,128)(2,1)S(1)}, bf16[3,32,1664]{2,1,0:T(8,128)(2,1)S(1)}, u32[]{:S(2)}, u32[]{:S(2)}) %collective-permute-start.21) | collective-permute-done | bytes 319520 | tf_op jit(solution)/shard_map/ppermute | solution.py:369
  204.3 3.3 %shard_map.115 = bf16[3,64,6400]{2,1,0:T(8,128)(2,1)} custom-call(bf16[3,32,1664]{2,1,0:T(8,128)(2,1)} %get-tuple-element.29.refs_0_, bf16[3,32,1664]{2,1,0:T(8,128)(2,1)} %get-tuple-element.30.refs_1_, bf16[3,32,1664]{2,1,0:T(8,128)(2,1)} %copy-done.6, bf16[3,32,1664]{2,1,0:T(8,128)(2,1)} %copy-done.9, bf16[3,32,1664]{2,1,0:T(8,128)(2,1)} %copy-done.10, ...), custom_call_target="tpu_custom_call" | custom-call | tf_op jit(solution)/shard_map/pallas_call | solution.py:490
  (75 shorter events, 13.8 us)
Async XLA Ops:
  45.7 3.3 %collective-permute-start = (bf16[256,128]{1,0:T(8,128)(2,1)}, bf16[256,128]{1,0:T(8,128)(2,1)S(1)}, u32[]{:S(2)}, u32[]{:S(2)}) collective-permute-start(bf16[256,128]{1,0:T(8,128)(2,1)} %get-tuple-element.20), channel_id=1, source_target_pairs={{0,8},{4,12},{8,0},{12,4},{16,24},{20,28},{24,16},{28,20},{32,40},... | collective-permute-start | bytes 196616 | tf_op jit(solution)/shard_map/ppermute | solution.py:374
  49.9 9.8 %collective-permute-start.2 = (bf16[2,256,128]{2,1,0:T(8,128)(2,1)S(1)}, bf16[2,256,128]{2,1,0:T(8,128)(2,1)S(1)}, u32[]{:S(2)}, u32[]{:S(2)}) collective-permute-start(bf16[2,256,128]{2,1,0:T(8,128)(2,1)S(1)} %get-tuple-element.32), channel_id=1, source_target_pairs={{0,32},{4,36},{8,40},{12,44},{16,48},{20,52},{24,56},{28,60},{32,0... | collective-permute-start | bytes 393224 | tf_op jit(solution)/shard_map/ppermute | solution.py:384
  52.7 12.2 %collective-permute-start.6 = (bf16[13,80,128]{2,1,0:T(8,128)(2,1)}, bf16[13,80,128]{2,1,0:T(8,128)(2,1)S(1)}, u32[]{:S(2)}, u32[]{:S(2)}) collective-permute-start(bf16[13,80,128]{2,1,0:T(8,128)(2,1)} %get-tuple-element.21.own), channel_id=1, source_target_pairs={{0,3},{1,0},{2,1},{3,2},{4,7},{5,4},{6,5},{7,6},{8,11},{9,8},{10,9... | collective-permute-start | bytes 798728 | tf_op jit(solution)/shard_map/ppermute | solution.py:369
  55.5 9.4 %collective-permute-start.5 = (bf16[13,80,128]{2,1,0:T(8,128)(2,1)}, bf16[13,80,128]{2,1,0:T(8,128)(2,1)S(1)}, u32[]{:S(2)}, u32[]{:S(2)}) collective-permute-start(bf16[13,80,128]{2,1,0:T(8,128)(2,1)} %get-tuple-element.21.own), channel_id=1, source_target_pairs={{0,2},{1,3},{2,0},{3,1},{4,6},{5,7},{6,4},{7,5},{8,10},{9,11},{10,... | collective-permute-start | bytes 798728 | tf_op jit(solution)/shard_map/ppermute | solution.py:369
  55.8 15.4 %collective-permute-start.4 = (bf16[13,80,128]{2,1,0:T(8,128)(2,1)}, bf16[13,80,128]{2,1,0:T(8,128)(2,1)S(1)}, u32[]{:S(2)}, u32[]{:S(2)}) collective-permute-start(bf16[13,80,128]{2,1,0:T(8,128)(2,1)} %get-tuple-element.21.own), channel_id=1, source_target_pairs={{0,1},{1,2},{2,3},{3,0},{4,5},{5,6},{6,7},{7,4},{8,9},{9,10},{10,1... | collective-permute-start | bytes 798728 | tf_op jit(solution)/shard_map/ppermute | solution.py:369
  56.5 6.5 %collective-permute-start.1 = (bf16[2,256,128]{2,1,0:T(8,128)(2,1)S(1)}, bf16[2,256,128]{2,1,0:T(8,128)(2,1)S(1)}, u32[]{:S(2)}, u32[]{:S(2)}) collective-permute-start(bf16[2,256,128]{2,1,0:T(8,128)(2,1)S(1)} %get-tuple-element.32), channel_id=1, source_target_pairs={{0,16},{4,20},{8,24},{12,28},{16,32},{20,36},{24,40},{28,44},{32,4... | collective-permute-start | bytes 393224 | tf_op jit(solution)/shard_map/ppermute | solution.py:384
  59.7 5.1 %collective-permute-start.3 = (bf16[2,256,128]{2,1,0:T(8,128)(2,1)S(1)}, bf16[2,256,128]{2,1,0:T(8,128)(2,1)S(1)}, u32[]{:S(2)}, u32[]{:S(2)}) collective-permute-start(bf16[2,256,128]{2,1,0:T(8,128)(2,1)S(1)} %get-tuple-element.32), channel_id=1, source_target_pairs={{0,48},{4,52},{8,56},{12,60},{16,0},{20,4},{24,8},{28,12},{32,16},... | collective-permute-start | bytes 393224 | tf_op jit(solution)/shard_map/ppermute | solution.py:384
  64.9 38.3 %copy-start = (bf16[4,2,256,128]{3,2,1,0:T(8,128)(2,1)}, bf16[4,2,256,128]{3,2,1,0:T(8,128)(2,1)S(1)}, u32[]{:S(2)}) copy-start(bf16[4,2,256,128]{3,2,1,0:T(8,128)(2,1)S(1)} %pad_maximum_fusion.refs_0_) | copy-start | bytes 1572868
  75.8 13.0 %collective-permute-start.8 = (bf16[4,2,256,128]{3,2,1,0:T(8,128)(2,1)S(1)}, bf16[4,2,256,128]{3,2,1,0:T(8,128)(2,1)S(1)}, u32[]{:S(2)}, u32[]{:S(2)}) collective-permute-start(bf16[4,2,256,128]{3,2,1,0:T(8,128)(2,1)S(1)} %pad_maximum_fusion.refs_0_), channel_id=1, source_target_pairs={{0,192},{4,196},{8,200},{12,204},{16,208},{20,212},{24,216},{28,22... | collective-permute-start | bytes 1572872 | tf_op jit(solution)/shard_map/ppermute | solution.py:384
  78.3 13.7 %collective-permute-start.7 = (bf16[4,2,256,128]{3,2,1,0:T(8,128)(2,1)S(1)}, bf16[4,2,256,128]{3,2,1,0:T(8,128)(2,1)S(1)}, u32[]{:S(2)}, u32[]{:S(2)}) collective-permute-start(bf16[4,2,256,128]{3,2,1,0:T(8,128)(2,1)S(1)} %pad_maximum_fusion.refs_0_), channel_id=1, source_target_pairs={{0,64},{4,68},{8,72},{12,76},{16,80},{20,84},{24,88},{28,92},{32,9... | collective-permute-start | bytes 1572872 | tf_op jit(solution)/shard_map/ppermute | solution.py:384
  78.3 23.8 %collective-permute-start.11 = (bf16[4,2,256,128]{3,2,1,0:T(8,128)(2,1)S(1)}, bf16[4,2,256,128]{3,2,1,0:T(8,128)(2,1)S(1)}, u32[]{:S(2)}, u32[]{:S(2)}) collective-permute-start(bf16[4,2,256,128]{3,2,1,0:T(8,128)(2,1)S(1)} %pad_maximum_fusion.refs_0_), channel_id=1, source_target_pairs={{0,4},{4,0},{8,12},{12,8},{16,20},{20,16},{24,28},{28,24},{32,36},... | collective-permute-start | bytes 1572872 | tf_op jit(solution)/shard_map/ppermute | solution.py:384
  88.8 14.4 %copy-start.1 = (bf16[4,2,256,128]{3,2,1,0:T(8,128)(2,1)}, bf16[4,2,256,128]{3,2,1,0:T(8,128)(2,1)S(1)}, u32[]{:S(2)}) copy-start(bf16[4,2,256,128]{3,2,1,0:T(8,128)(2,1)S(1)} %collective-permute-done.8.refs_2_) | copy-start | bytes 1572868
  88.9 6.8 %collective-permute-start.10 = (bf16[2,2,256,128]{3,2,1,0:T(8,128)(2,1)S(1)}, bf16[2,2,256,128]{3,2,1,0:T(8,128)(2,1)S(1)}, u32[]{:S(2)}, u32[]{:S(2)}) collective-permute-start(bf16[2,2,256,128]{3,2,1,0:T(8,128)(2,1)S(1)} %slice.9), channel_id=1, source_target_pairs={{0,192},{4,196},{8,200},{12,204},{16,208},{20,212},{24,216},{28,22... | collective-permute-start | bytes 786440 | tf_op jit(solution)/shard_map/ppermute | solution.py:384
  92.0 11.2 %copy-start.2 = (bf16[4,2,256,128]{3,2,1,0:T(8,128)(2,1)}, bf16[4,2,256,128]{3,2,1,0:T(8,128)(2,1)S(1)}, u32[]{:S(2)}) copy-start(bf16[4,2,256,128]{3,2,1,0:T(8,128)(2,1)S(1)} %collective-permute-done.7.refs_1_) | copy-start | bytes 1572868
  92.0 6.9 %collective-permute-start.9 = (bf16[2,2,256,128]{3,2,1,0:T(8,128)(2,1)S(1)}, bf16[2,2,256,128]{3,2,1,0:T(8,128)(2,1)S(1)}, u32[]{:S(2)}, u32[]{:S(2)}) collective-permute-start(bf16[2,2,256,128]{3,2,1,0:T(8,128)(2,1)S(1)} %slice.8), channel_id=1, source_target_pairs={{0,64},{4,68},{8,72},{12,76},{16,80},{20,84},{24,88},{28,92},{32,9... | collective-permute-start | bytes 786440 | tf_op jit(solution)/shard_map/ppermute | solution.py:384
  92.1 11.1 %collective-permute-start.13 = (bf16[4,2,256,128]{3,2,1,0:T(8,128)(2,1)S(1)}, bf16[4,2,256,128]{3,2,1,0:T(8,128)(2,1)S(1)}, u32[]{:S(2)}, u32[]{:S(2)}) collective-permute-start(bf16[4,2,256,128]{3,2,1,0:T(8,128)(2,1)S(1)} %collective-permute-done.8.refs_2_), channel_id=1, source_target_pairs={{0,4},{4,0},{8,12},{12,8},{16,20},{20,16},{24,28},{28,24},{32,36},... | collective-permute-start | bytes 1572872 | tf_op jit(solution)/shard_map/ppermute | solution.py:384
  94.6 8.6 %collective-permute-start.12 = (bf16[4,2,256,128]{3,2,1,0:T(8,128)(2,1)S(1)}, bf16[4,2,256,128]{3,2,1,0:T(8,128)(2,1)S(1)}, u32[]{:S(2)}, u32[]{:S(2)}) collective-permute-start(bf16[4,2,256,128]{3,2,1,0:T(8,128)(2,1)S(1)} %collective-permute-done.7.refs_1_), channel_id=1, source_target_pairs={{0,4},{4,0},{8,12},{12,8},{16,20},{20,16},{24,28},{28,24},{32,36},... | collective-permute-start | bytes 1572872 | tf_op jit(solution)/shard_map/ppermute | solution.py:384
  95.7 7.6 %copy-start.18 = (bf16[2,2,256,128]{3,2,1,0:T(8,128)(2,1)}, bf16[2,2,256,128]{3,2,1,0:T(8,128)(2,1)S(1)}, u32[]{:S(2)}) copy-start(bf16[2,2,256,128]{3,2,1,0:T(8,128)(2,1)S(1)} %collective-permute-done.10.refs_4_) | copy-start | bytes 786436
  95.7 6.4 %collective-permute-start.15 = (bf16[2,2,256,128]{3,2,1,0:T(8,128)(2,1)S(1)}, bf16[2,2,256,128]{3,2,1,0:T(8,128)(2,1)S(1)}, u32[]{:S(2)}, u32[]{:S(2)}) collective-permute-start(bf16[2,2,256,128]{3,2,1,0:T(8,128)(2,1)S(1)} %collective-permute-done.10.refs_4_), channel_id=1, source_target_pairs={{0,4},{4,0},{8,12},{12,8},{16,20},{20,16},{24,28},{28,24},{32,36},... | collective-permute-start | bytes 786440 | tf_op jit(solution)/shard_map/ppermute | solution.py:384
  98.9 4.3 %collective-permute-start.14 = (bf16[2,2,256,128]{3,2,1,0:T(8,128)(2,1)S(1)}, bf16[2,2,256,128]{3,2,1,0:T(8,128)(2,1)S(1)}, u32[]{:S(2)}, u32[]{:S(2)}) collective-permute-start(bf16[2,2,256,128]{3,2,1,0:T(8,128)(2,1)S(1)} %collective-permute-done.9.refs_3_), channel_id=1, source_target_pairs={{0,4},{4,0},{8,12},{12,8},{16,20},{20,16},{24,28},{28,24},{32,36},... | collective-permute-start | bytes 786440 | tf_op jit(solution)/shard_map/ppermute | solution.py:384
  130.3 9.0 %collective-permute-start.16 = (bf16[13,80,128]{2,1,0:T(8,128)(2,1)}, bf16[13,80,128]{2,1,0:T(8,128)(2,1)S(1)}, u32[]{:S(2)}, u32[]{:S(2)}) collective-permute-start(bf16[13,80,128]{2,1,0:T(8,128)(2,1)} %get-tuple-element.25), channel_id=1, source_target_pairs={{0,1},{1,2},{2,3},{3,0},{4,5},{5,6},{6,7},{7,4},{8,9},{9,10},{10,1... | collective-permute-start | bytes 798728 | tf_op jit(solution)/shard_map/ppermute | solution.py:369
  131.0 14.8 %collective-permute-start.17 = (bf16[13,80,128]{2,1,0:T(8,128)(2,1)}, bf16[13,80,128]{2,1,0:T(8,128)(2,1)S(1)}, u32[]{:S(2)}, u32[]{:S(2)}) collective-permute-start(bf16[13,80,128]{2,1,0:T(8,128)(2,1)} %get-tuple-element.26), channel_id=1, source_target_pairs={{0,2},{1,3},{2,0},{3,1},{4,6},{5,7},{6,4},{7,5},{8,10},{9,11},{10,... | collective-permute-start | bytes 798728 | tf_op jit(solution)/shard_map/ppermute | solution.py:369
  133.8 12.1 %collective-permute-start.18 = (bf16[13,80,128]{2,1,0:T(8,128)(2,1)}, bf16[13,80,128]{2,1,0:T(8,128)(2,1)S(1)}, u32[]{:S(2)}, u32[]{:S(2)}) collective-permute-start(bf16[13,80,128]{2,1,0:T(8,128)(2,1)} %get-tuple-element.27), channel_id=1, source_target_pairs={{0,3},{1,0},{2,1},{3,2},{4,7},{5,4},{6,5},{7,6},{8,11},{9,8},{10,9... | collective-permute-start | bytes 798728 | tf_op jit(solution)/shard_map/ppermute | solution.py:369
  178.9 10.3 %collective-permute-start.19 = (bf16[3,32,1664]{2,1,0:T(8,128)(2,1)}, bf16[3,32,1664]{2,1,0:T(8,128)(2,1)S(1)}, u32[]{:S(2)}, u32[]{:S(2)}) collective-permute-start(bf16[3,32,1664]{2,1,0:T(8,128)(2,1)} %get-tuple-element.29.refs_0_), channel_id=1, source_target_pairs={{0,1},{1,2},{2,3},{3,0},{4,5},{5,6},{6,7},{7,4},{8,9},{9,10},{10,1... | collective-permute-start | bytes 958472 | tf_op jit(solution)/shard_map/ppermute | solution.py:369
  179.4 9.8 %collective-permute-start.22 = (bf16[3,32,1664]{2,1,0:T(8,128)(2,1)}, bf16[3,32,1664]{2,1,0:T(8,128)(2,1)S(1)}, u32[]{:S(2)}, u32[]{:S(2)}) collective-permute-start(bf16[3,32,1664]{2,1,0:T(8,128)(2,1)} %get-tuple-element.30.refs_1_), channel_id=1, source_target_pairs={{0,3},{1,0},{2,1},{3,2},{4,7},{5,4},{6,5},{7,6},{8,11},{9,8},{10,9... | collective-permute-start | bytes 958472 | tf_op jit(solution)/shard_map/ppermute | solution.py:369
  181.6 13.5 %collective-permute-start.24 = (bf16[3,32,1664]{2,1,0:T(8,128)(2,1)}, bf16[3,32,1664]{2,1,0:T(8,128)(2,1)S(1)}, u32[]{:S(2)}, u32[]{:S(2)}) collective-permute-start(bf16[3,32,1664]{2,1,0:T(8,128)(2,1)} %get-tuple-element.29.refs_0_), channel_id=1, source_target_pairs={{0,3},{1,0},{2,1},{3,2},{4,7},{5,4},{6,5},{7,6},{8,11},{9,8},{10,9... | collective-permute-start | bytes 958472 | tf_op jit(solution)/shard_map/ppermute | solution.py:369
  182.4 13.6 %collective-permute-start.20 = (bf16[3,32,1664]{2,1,0:T(8,128)(2,1)}, bf16[3,32,1664]{2,1,0:T(8,128)(2,1)S(1)}, u32[]{:S(2)}, u32[]{:S(2)}) collective-permute-start(bf16[3,32,1664]{2,1,0:T(8,128)(2,1)} %get-tuple-element.30.refs_1_), channel_id=1, source_target_pairs={{0,1},{1,2},{2,3},{3,0},{4,5},{5,6},{6,7},{7,4},{8,9},{9,10},{10,1... | collective-permute-start | bytes 958472 | tf_op jit(solution)/shard_map/ppermute | solution.py:369
  189.2 13.7 %copy-start.6 = (bf16[3,32,1664]{2,1,0:T(8,128)(2,1)}, bf16[3,32,1664]{2,1,0:T(8,128)(2,1)S(1)}, u32[]{:S(2)}) copy-start(bf16[3,32,1664]{2,1,0:T(8,128)(2,1)S(1)} %collective-permute-done.19.refs_2_) | copy-start | bytes 958468
  189.2 13.7 %collective-permute-start.21 = (bf16[3,32,1664]{2,1,0:T(8,128)(2,1)S(1)}, bf16[3,32,1664]{2,1,0:T(8,128)(2,1)S(1)}, u32[]{:S(2)}, u32[]{:S(2)}) collective-permute-start(bf16[3,32,1664]{2,1,0:T(8,128)(2,1)S(1)} %collective-permute-done.19.refs_2_), channel_id=1, source_target_pairs={{0,1},{1,2},{2,3},{3,0},{4,5},{5,6},{6,7},{7,4},{8,9},{9,10},{10,1... | collective-permute-start | bytes 958472 | tf_op jit(solution)/shard_map/ppermute | solution.py:369
  189.2 13.7 %copy-start.7 = (bf16[3,32,1664]{2,1,0:T(8,128)(2,1)}, bf16[3,32,1664]{2,1,0:T(8,128)(2,1)S(1)}, u32[]{:S(2)}) copy-start(bf16[3,32,1664]{2,1,0:T(8,128)(2,1)S(1)} %collective-permute-done.22.refs_7_) | copy-start | bytes 958468
  189.2 13.7 %collective-permute-start.23 = (bf16[3,32,1664]{2,1,0:T(8,128)(2,1)S(1)}, bf16[3,32,1664]{2,1,0:T(8,128)(2,1)S(1)}, u32[]{:S(2)}, u32[]{:S(2)}) collective-permute-start(bf16[3,32,1664]{2,1,0:T(8,128)(2,1)S(1)} %collective-permute-done.22.refs_7_), channel_id=1, source_target_pairs={{0,3},{1,0},{2,1},{3,2},{4,7},{5,4},{6,5},{7,6},{8,11},{9,8},{10,9... | collective-permute-start | bytes 958472 | tf_op jit(solution)/shard_map/ppermute | solution.py:369
  195.1 7.8 %copy-start.8 = (bf16[3,32,1664]{2,1,0:T(8,128)(2,1)}, bf16[3,32,1664]{2,1,0:T(8,128)(2,1)S(1)}, u32[]{:S(2)}) copy-start(bf16[3,32,1664]{2,1,0:T(8,128)(2,1)S(1)} %collective-permute-done.24.refs_6_) | copy-start | bytes 958468
  (15 other events, 38.9 us)
